TPU v7x, 256 devices: a whole 4x4x8 slice. The times are simulated.
256 devices in a mesh: row: 16 (over x, y_lo, core), col: 16 (over y_hi, z).
Axes of the slice: x: 4, y: 4 (y_hi: 2, y_lo: 2; y = y_hi * 2 + y_lo), z: 8, core: 2. Of those that a mesh axis runs over, the one named last changes fastest.
Arguments:
- start_block: float32 [64, 65536], P(None, ('col', 'row')), may hold values from -6 to 6
- tile_values: bfloat16 [16, 16, 80, 256, 256], P('row', 'col'), may hold values from 0.0001 to 1
- tile_rows: int32 [16, 16, 80], P('row', 'col'), may hold values from 0 to 15, as said below
- tile_cols: int32 [16, 16, 80], P('row', 'col'), may hold values from 0 to 15, as said below
- tile_count: int32 [16, 16], P('row', 'col'), may hold values from 16 to 80, as said below
Outputs:
- filtered: float32 [64, 65536], P(None, ('col', 'row'))
- preceding: float32 [64, 65536], P(None, ('col', 'row'))
Inputs may be any that keep to these rules, and one draw needn't show every extreme that they name: `tile_count`: the busiest device has exactly 80 live slots. `tile_rows`: slot k below max(16, 16) lies at tile row k % 16; slots at the same coordinates add. `tile_cols`: slot k below max(16, 16) lies at tile column k % 16.
All inputs are finite; a program needn't handle non-finite values.
Results may differ from a plain program's by a relative error of at most 0.0028.
Values may be sent and summed in bfloat16 or wider, within the bound.
No kernel may reach another device: no remote copies, remote signals or barrier semaphores. Data moves between devices by JAX's collectives and lax.ppermute only.
A program may use at most 64 MiB of HBM per device.

v0:
```python
import jax
import jax.numpy as jnp
from jax import lax
from jax.sharding import PartitionSpec as P

DEGREE = 3


filter_center = 0.4
filter_half = 0.4


def on_device(start_block, tile_values, tile_rows, tile_cols, tile_count):
    local_tiles = tile_values[0, 0]
    local_rows = tile_rows[0, 0]
    local_cols = tile_cols[0, 0]
    live_count = tile_count[0, 0]
    tile_width = local_tiles.shape[-1]
    slot_count = local_tiles.shape[0]
    piece_len = start_block.shape[1]
    column_count = start_block.shape[0]
    tile_rows_here = piece_len * lax.axis_size("col") // tile_width
    tile_cols_here = piece_len * lax.axis_size("row") // tile_width
    live_mask = (jnp.arange(slot_count) < live_count).astype(jnp.float32)
    onehot_rows = (local_rows[:, None] == jnp.arange(tile_rows_here)[None, :]).astype(
        jnp.float32
    ) * live_mask[:, None]
    onehot_cols = (local_cols[:, None] == jnp.arange(tile_cols_here)[None, :]).astype(
        jnp.float32
    ) * live_mask[:, None]

    def forward(vec_panel):
        gathered = jnp.take(
            vec_panel.reshape(column_count, tile_cols_here, tile_width), local_cols, axis=1
        )
        contrib = jnp.einsum(
            "ckj,kij->cki", gathered, local_tiles, preferred_element_type=jnp.float32
        )
        placed = jnp.einsum("cki,kr->cri", contrib, onehot_rows, precision=lax.Precision.HIGHEST)
        return placed.reshape(column_count, tile_rows_here * tile_width)

    def backward(vec_panel):
        gathered = jnp.take(
            vec_panel.reshape(column_count, tile_rows_here, tile_width), local_rows, axis=1
        )
        contrib = jnp.einsum(
            "cki,kij->ckj", gathered, local_tiles, preferred_element_type=jnp.float32
        )
        placed = jnp.einsum("ckj,kr->crj", contrib, onehot_cols, precision=lax.Precision.HIGHEST)
        return placed.reshape(column_count, tile_cols_here * tile_width)

    row_sums = jnp.sum(local_tiles, axis=2, dtype=jnp.float32)
    col_sums = jnp.sum(local_tiles, axis=1, dtype=jnp.float32)
    row_terms = jnp.einsum(
        "ki,kr->ri", row_sums, onehot_rows, precision=lax.Precision.HIGHEST
    ).reshape(1, tile_rows_here * tile_width)
    col_terms = jnp.einsum(
        "kj,kr->rj", col_sums, onehot_cols, precision=lax.Precision.HIGHEST
    ).reshape(1, tile_cols_here * tile_width)

    def sum_rows(term):
        return lax.psum_scatter(term, "col", scatter_dimension=1, tiled=True)

    def sum_cols(term):
        return lax.psum_scatter(term, "row", scatter_dimension=1, tiled=True)

    def widen_cols(vector):
        return lax.all_gather(vector, "row", axis=1, tiled=True)

    def widen_rows(vector):
        return lax.all_gather(vector, "col", axis=1, tiled=True)

    row_degree = sum_rows(row_terms)[0]
    col_degree = sum_cols(col_terms)[0]
    col_scale = lax.rsqrt(col_degree)
    row_inverse = 1.0 / row_degree

    def apply_filter(vector):
        scaled = (col_scale * vector).astype(jnp.bfloat16)
        mixed = sum_rows(forward(widen_cols(scaled)))
        weighted = (mixed * row_inverse).astype(jnp.bfloat16)
        back = sum_cols(backward(widen_rows(weighted)))
        return (col_scale * back - filter_center * vector) / filter_half

    previous = start_block
    current = apply_filter(start_block)
    for step_index in range(DEGREE - 1):
        previous, current = (current, 2.0 * apply_filter(current) - previous)
    return (current, previous)


def solution(mesh):
    return jax.shard_map(
        on_device,
        mesh=mesh,
        in_specs=(
            P(None, ("col", "row")),
            P("row", "col", None, None, None),
            P("row", "col", None),
            P("row", "col", None),
            P("row", "col"),
        ),
        out_specs=(P(None, ("col", "row")), P(None, ("col", "row"))),
        check_vma=False,
    )
```

profile of v0, /device:TPU:8, one launch (start us, length us, event | category | flops | bytes accessed | tf_op | source)
XLA Modules:
  0.0 1311.0 jit_solution(13290661319704265347)
XLA Ops:
  7.2 0.0 reduce-scatter.25.cloned.1.call-start
  7.9 7.8 convert_reduce_fusion
  15.7 0.1 convolution_bitcast_fusion.1
  15.9 0.6 copy.42
  16.6 1.4 bitcast_bitcast_fusion.1
  18.0 0.0 reduce-scatter.25.cloned.1.call-update
  18.0 0.0 reduce-scatter.27.cloned.1.call-start
  18.1 0.1 convolution_bitcast_fusion
  18.3 0.6 copy.45
  18.9 1.5 bitcast_bitcast_fusion
  20.4 0.0 reduce-scatter.13.cloned.1.call-start
  20.5 62.7 %reduce-scatter.25.cloned.1.call-done = f32[256,1]{1,0:T(8,128)} async-done(((f32[4096,1]{1,0:T(8,128)}), f32[256,1]{1,0:T(8,128)}) %reduce-scatter.25.cloned.1.call-update) | async-done | bytes 1040
  83.3 0.9 rsqrt_bitcast_fusion
  84.2 0.1 copy.51
  84.3 22.3 %all_gather.18 = bf16[64,4096]{1,0:T(8,128)(2,1)S(1)} all-gather(bf16[64,256]{1,0:T(8,128)(2,1)S(1)} %multiply_convert_fusion.5), channel_id=1, replica_groups=mesh['row'=16,'col'=16] {'row'}, dimensions={1}, use_global_device_ids=true | all-gather | bytes 557056 | tf_op jit(solution)/shard_map/all_gather | solution.py:68
  106.6 0.7 gather_fusion
  107.4 7.3 fusion.42
  114.7 5.4 fusion.22
  120.1 1.6 copy.43
  121.7 0.0 reduce-scatter.15.cloned.1.call-start
  121.8 171.3 %reduce-scatter.27.cloned.1.call-done = f32[256,1]{1,0:T(8,128)} async-done(((f32[4096,1]{1,0:T(8,128)}), f32[256,1]{1,0:T(8,128)}) %reduce-scatter.27.cloned.1.call-update) | async-done | bytes 1040
  293.1 0.9 divide_bitcast_fusion
  294.0 0.1 copy.52
  294.1 200.0 %reduce-scatter.13.cloned.1.call-done = f32[64,256]{1,0:T(8,128)} async-done(((f32[64,4096]{1,0:T(8,128)}), f32[64,256]{1,0:T(8,128)}) %reduce-scatter.13.cloned.1.call-update) | async-done | bytes 65552 | tf_op jit(solution)/shard_map/reduce_scatter | solution.py:62
  494.0 0.8 multiply_convert_fusion.4
  494.9 41.2 %all_gather.19 = bf16[64,4096]{1,0:T(8,128)(2,1)S(1)} all-gather(bf16[64,256]{1,0:T(8,128)(2,1)S(1)} %multiply_convert_fusion.4), channel_id=1, replica_groups=mesh['row'=16,'col'=16] {'col'}, dimensions={1}, use_global_device_ids=true | all-gather | bytes 557056 | tf_op jit(solution)/shard_map/all_gather | solution.py:71
  536.1 0.7 gather_fusion.1
  536.9 6.0 fusion.47
  542.9 5.4 fusion.20
  548.3 1.6 copy.46
  549.9 0.0 reduce-scatter.17.cloned.1.call-start
  550.0 56.4 %reduce-scatter.15.cloned.1.call-done = f32[64,256]{1,0:T(8,128)} async-done(((f32[64,4096]{1,0:T(8,128)}), f32[64,256]{1,0:T(8,128)}) %reduce-scatter.15.cloned.1.call-update) | async-done | bytes 65552 | tf_op jit(solution)/shard_map/reduce_scatter | solution.py:65
  606.4 0.9 multiply_convert_fusion.3
  607.2 22.2 %all_gather.20 = bf16[64,4096]{1,0:T(8,128)(2,1)S(1)} all-gather(bf16[64,256]{1,0:T(8,128)(2,1)S(1)} %multiply_convert_fusion.3), channel_id=1, replica_groups=mesh['row'=16,'col'=16] {'row'}, dimensions={1}, use_global_device_ids=true | all-gather | bytes 557056 | tf_op jit(solution)/shard_map/all_gather | solution.py:68
  629.4 0.7 gather_fusion.2
  630.2 7.3 fusion.52
  637.4 5.4 fusion.18
  642.9 1.6 copy.47
  644.5 0.0 reduce-scatter.19.cloned.1.call-start
  644.5 197.4 %reduce-scatter.17.cloned.1.call-done = f32[64,256]{1,0:T(8,128)} async-done(((f32[64,4096]{1,0:T(8,128)}), f32[64,256]{1,0:T(8,128)}) %reduce-scatter.17.cloned.1.call-update) | async-done | bytes 65552 | tf_op jit(solution)/shard_map/reduce_scatter | solution.py:62
  841.9 0.8 multiply_convert_fusion.2
  842.8 41.5 %all_gather.21 = bf16[64,4096]{1,0:T(8,128)(2,1)S(1)} all-gather(bf16[64,256]{1,0:T(8,128)(2,1)S(1)} %multiply_convert_fusion.2), channel_id=1, replica_groups=mesh['row'=16,'col'=16] {'col'}, dimensions={1}, use_global_device_ids=true | all-gather | bytes 557056 | tf_op jit(solution)/shard_map/all_gather | solution.py:71
  884.3 0.7 gather_fusion.3
  885.1 6.0 fusion.57
  891.0 5.4 fusion.16
  896.5 1.6 copy.48
  898.1 0.0 reduce-scatter.21.cloned.1.call-start
  898.1 56.5 %reduce-scatter.19.cloned.1.call-done = f32[64,256]{1,0:T(8,128)} async-done(((f32[64,4096]{1,0:T(8,128)}), f32[64,256]{1,0:T(8,128)}) %reduce-scatter.19.cloned.1.call-update) | async-done | bytes 65552 | tf_op jit(solution)/shard_map/reduce_scatter | solution.py:65
  954.6 0.9 multiply_convert_fusion.1
  955.5 22.0 %all_gather.22 = bf16[64,4096]{1,0:T(8,128)(2,1)S(1)} all-gather(bf16[64,256]{1,0:T(8,128)(2,1)S(1)} %get-tuple-element.5), channel_id=1, replica_groups=mesh['row'=16,'col'=16] {'row'}, dimensions={1}, use_global_device_ids=true | all-gather | bytes 557056 | tf_op jit(solution)/shard_map/all_gather | solution.py:68
  977.6 0.7 gather_fusion.4
  978.4 7.3 fusion.62
  985.6 5.4 fusion.14
  991.0 1.6 copy.49
  992.7 0.0 reduce-scatter.23.cloned.1.call-start
  992.7 197.5 %reduce-scatter.21.cloned.1.call-done = f32[64,256]{1,0:T(8,128)} async-done(((f32[64,4096]{1,0:T(8,128)}), f32[64,256]{1,0:T(8,128)}) %reduce-scatter.21.cloned.1.call-update) | async-done | bytes 65552 | tf_op jit(solution)/shard_map/reduce_scatter | solution.py:62
  1190.2 0.8 multiply_convert_fusion
  1191.0 41.2 %all_gather.23 = bf16[64,4096]{1,0:T(8,128)(2,1)S(1)} all-gather(bf16[64,256]{1,0:T(8,128)(2,1)S(1)} %multiply_convert_fusion), channel_id=1, replica_groups=mesh['row'=16,'col'=16] {'col'}, dimensions={1}, use_global_device_ids=true | all-gather | bytes 557056 | tf_op jit(solution)/shard_map/all_gather | solution.py:71
  1232.3 0.7 gather_fusion.5
  1233.0 6.0 fusion.67
  1239.0 5.4 fusion.12
  1244.4 1.6 copy.50
  1246.0 56.4 %reduce-scatter.23.cloned.1.call-done = f32[64,256]{1,0:T(8,128)} async-done(((f32[64,4096]{1,0:T(8,128)}), f32[64,256]{1,0:T(8,128)}) %reduce-scatter.23.cloned.1.call-update) | async-done | bytes 65552 | tf_op jit(solution)/shard_map/reduce_scatter | solution.py:65
  1302.4 1.5 multiply_subtract_fusion
  (34 shorter events, 0.5 us)
Async XLA Ops:
  7.2 76.1 %reduce-scatter.25.cloned.1.call-start = ((), (), s32[]{:S(2)}) async-start(), calls=%async_computation.14 | async-start | bytes 2228224
  7.9 7.8 copy-start.4
  16.5 1.5 copy-start.3
  18.0 275.0 %reduce-scatter.27.cloned.1.call-start = ((), (), s32[]{:S(2)}) async-start(), calls=%async_computation.15 | async-start | bytes 2228224
  18.9 65.4 %copy-start = (f32[64,256]{1,0:T(8,128)S(1)}, f32[64,256]{1,0:T(8,128)}, u32[]{:S(2)}) copy-start(f32[64,256]{1,0:T(8,128)} %param.7) | copy-start | bytes 196612
  20.4 473.6 %reduce-scatter.13.cloned.1.call-start = ((), (), s32[]{:S(2)}) async-start(), calls=%async_computation.8 | async-start | bytes 1114112 | tf_op jit(solution)/shard_map/reduce_scatter | solution.py:62
  121.7 484.7 %reduce-scatter.15.cloned.1.call-start = ((), (), s32[]{:S(2)}) async-start(), calls=%async_computation.9 | async-start | bytes 1114112 | tf_op jit(solution)/shard_map/reduce_scatter | solution.py:65
  549.9 292.0 %reduce-scatter.17.cloned.1.call-start = ((), (), s32[]{:S(2)}) async-start(), calls=%async_computation.10 | async-start | bytes 1114112 | tf_op jit(solution)/shard_map/reduce_scatter | solution.py:62
  644.5 310.2 %reduce-scatter.19.cloned.1.call-start = ((), (), s32[]{:S(2)}) async-start(), calls=%async_computation.11 | async-start | bytes 1114112 | tf_op jit(solution)/shard_map/reduce_scatter | solution.py:65
  896.4 58.2 %copy-start.1 = (f32[64,256]{1,0:T(8,128)S(1)}, f32[64,256]{1,0:T(8,128)}, u32[]{:S(2)}) copy-start(f32[64,256]{1,0:T(8,128)} %reduce-scatter.15.cloned.1.call-done) | copy-start | bytes 196612
  898.1 292.1 %reduce-scatter.21.cloned.1.call-start = ((), (), s32[]{:S(2)}) async-start(), calls=%async_computation.12 | async-start | bytes 1114112 | tf_op jit(solution)/shard_map/reduce_scatter | solution.py:62
  955.5 346.9 %copy-start.2 = (f32[64,256]{1,0:T(8,128)}, f32[64,256]{1,0:T(8,128)S(1)}, u32[]{:S(2)}) copy-start(f32[64,256]{1,0:T(8,128)S(1)} %get-tuple-element.6) | copy-start | bytes 196612
  992.7 309.7 %reduce-scatter.23.cloned.1.call-start = ((), (), s32[]{:S(2)}) async-start(), calls=%async_computation.13 | async-start | bytes 1114112 | tf_op jit(solution)/shard_map/reduce_scatter | solution.py:65
Sparse Core Ops, SparseCore 0:
  18.1 65.0 reduce-scatter.24
  87.1 205.8 reduce-scatter.26
  296.9 197.1 reduce-scatter.12
  550.0 56.3 reduce-scatter.14
  644.6 197.2 reduce-scatter.16
  898.2 56.3 reduce-scatter.18
  992.8 197.3 reduce-scatter.20
  1246.1 56.2 reduce-scatter.22
where the time goes:
time: 1320 us; the launch traced here: 1310 us
  waiting for transfers between devices  998 us (76%)
  blocking collectives  190 us (14%)
  matrix products  72.5 us (5%)
  local copies, waits for them, and re-layouts  19.6 us (1%)
  between operations  15.3 us (1%)
  other arithmetic  14.6 us (1%)
    reduce_scatter x3, waiting for transfers between devices, sum_rows(): return lax.psum_scatter(term, 'col', scatter_dimension=1, tiled=True)  595 us
    unnamed x10, waiting for transfers between devices  234 us
    reduce_scatter x3, waiting for transfers between devices, sum_cols(): return lax.psum_scatter(term, 'row', scatter_dimension=1, tiled=True)  169 us
    all_gather x3, blocking collectives, widen_rows(): return lax.all_gather(vector, 'col', axis=1, tiled=True)  124 us
    all_gather x3, blocking collectives, widen_cols(): return lax.all_gather(vector, 'row', axis=1, tiled=True)  66.5 us
  transfers between devices with their start and end apart: 8, of which 8 were waited for; matrix products, arithmetic and copies ran while one was open for 1% of the time, Pallas kernels for 0%

commit v1 on v0

v1 whole, which is shorter than its diff:
```python
import functools

import jax
import jax.numpy as jnp
from jax import lax
from jax.experimental import pallas as pl
from jax.experimental.pallas import tpu as pltpu
from jax.sharding import PartitionSpec as P

DEGREE = 3
GROUP = 8

filter_center = 0.4
filter_half = 0.4

bf16, f32 = jnp.bfloat16, jnp.float32


def split_sums(sums):
    place = lax.broadcasted_iota(jnp.int32, sums.shape, 0)
    high = sums.astype(bf16).astype(f32)
    middle = (sums - high).astype(bf16).astype(f32)
    low = sums - high - middle
    return jnp.where(place == 0, high, jnp.where(place == 1, middle, jnp.where(place == 2, low, 0.0)))


def spread_kernel(transposed, degree_rows, count_ref, take_ref, put_ref, source_ref, tiles_ref, out_ref, total_ref):
    cover = total_ref.shape[0]
    slots = tiles_ref.shape[0]
    count = count_ref[0, 0]
    contract = (((1,), (1 if transposed else 0,)), ((), ()))

    def product(slot, take):
        return lax.dot_general(source_ref[take], tiles_ref[slot], contract, preferred_element_type=f32)

    for slot in range(cover):
        total_ref[slot] = product(slot, slot)

    def step(index, carry):
        first = cover + index * GROUP
        places, terms = [], []
        for offset in range(GROUP):
            slot = jnp.minimum(first + offset, slots - 1)
            term = product(slot, take_ref[0, slot])
            places.append(put_ref[0, slot])
            terms.append(jnp.where(first + offset < count, term, 0.0))
        for place, term in zip(places, terms):
            total_ref[place] += term
        return carry

    lax.fori_loop(0, (count - cover + GROUP - 1) // GROUP, step, 0)
    if degree_rows:
        vectors = total_ref.shape[1] - degree_rows
        out_ref[:, :vectors] = total_ref[:, :vectors].astype(out_ref.dtype)
        for place in range(cover):
            out_ref[place, vectors:] = split_sums(total_ref[place, vectors:]).astype(out_ref.dtype)
    else:
        out_ref[...] = total_ref[...].astype(out_ref.dtype)


def spread_tiles(source, tiles, take, put, count, transposed, dtype=bf16, degree_rows=0):
    smem = pl.BlockSpec(memory_space=pltpu.SMEM)
    vmem = pl.BlockSpec(memory_space=pltpu.VMEM)
    flops = 2 * tiles.size * source.shape[1]
    return pl.pallas_call(
        functools.partial(spread_kernel, transposed, degree_rows),
        out_shape=jax.ShapeDtypeStruct(source.shape, dtype),
        in_specs=[smem, smem, smem, vmem, vmem],
        out_specs=vmem,
        scratch_shapes=[pltpu.VMEM(source.shape, f32)],
        compiler_params=pltpu.CompilerParams(vmem_limit_bytes=16 * 2**20),
        cost_estimate=pl.CostEstimate(flops=flops, bytes_accessed=source.size * 4, transcendentals=0),
    )(count, take, put, source, tiles)


def on_device(start_block, tile_values, tile_rows, tile_cols, tile_count):
    vectors, piece = start_block.shape
    tiles = pltpu.with_memory_space_constraint(tile_values[0, 0], pltpu.VMEM)
    rows, cols = tile_rows[0], tile_cols[0]
    row_parts, col_parts = lax.axis_size("col"), lax.axis_size("row")

    def to_all(block, axis, parts):
        return lax.all_to_all(jnp.broadcast_to(block[None], (parts, *block.shape)), axis, 0, 0)

    def sum_parts(parts, axis):
        return jnp.sum(lax.all_to_all(parts, axis, 0, 0).astype(f32), axis=0)

    ones = jnp.ones((row_parts, 16, piece), bf16)
    col_terms = spread_tiles(ones, tiles, rows, cols, tile_count, False, dtype=f32)
    col_degree = sum_parts(col_terms[:, :8], "row")[0]
    col_scale = lax.rsqrt(col_degree)

    def forward(scaled, row_inverse):
        gathered = to_all(scaled, "row", col_parts)
        if row_inverse is None:
            gathered = jnp.concatenate([gathered, jnp.ones((col_parts, 16, piece), bf16)], axis=1)
            mixed = spread_tiles(gathered, tiles, cols, rows, tile_count, True, degree_rows=16)
            mixed = sum_parts(mixed, "col")
            row_inverse = 1.0 / (mixed[vectors] + mixed[vectors + 1] + mixed[vectors + 2])
            return mixed[:vectors], row_inverse
        mixed = spread_tiles(gathered, tiles, cols, rows, tile_count, True)
        return sum_parts(mixed, "col"), row_inverse

    def backward(weighted):
        gathered = to_all(weighted, "col", row_parts)
        return sum_parts(spread_tiles(gathered, tiles, rows, cols, tile_count, False), "row")

    def apply_filter(vector, row_inverse):
        scaled = (col_scale * vector).astype(bf16)
        mixed, row_inverse = forward(scaled, row_inverse)
        weighted = (mixed * row_inverse).astype(bf16)
        back = backward(weighted)
        return (col_scale * back - filter_center * vector) / filter_half, row_inverse

    previous = start_block
    current, row_inverse = apply_filter(start_block, None)
    for _ in range(DEGREE - 1):
        following, row_inverse = apply_filter(current, row_inverse)
        previous, current = current, 2.0 * following - previous
    return current, previous


def solution(mesh):
    return jax.shard_map(
        on_device,
        mesh=mesh,
        in_specs=(
            P(None, ("col", "row")),
            P("row", "col", None, None, None),
            P("row", "col", None),
            P("row", "col", None),
            P("row", "col"),
        ),
        out_specs=(P(None, ("col", "row")), P(None, ("col", "row"))),
        check_vma=False,
    )
```

time: 1320 us -> 267 us (0.20)
  waiting for transfers between devices: 998 us -> 9.34 us
  matrix products: 72.5 us -> 0 us
  blocking collectives: 190 us -> 219 us
  between operations: 15.3 us -> 1.59 us
  other arithmetic: 14.6 us -> 1.23 us
    reduce_scatter x6 -> x0, waiting for transfers between devices: 764 us -> none  [the longest x3 595 us: sum_rows(): return lax.psum_scatter(term, 'col', scatter_dimension=1, tiled=True)]
    unnamed x10 -> x0, waiting for transfers between devices: 234 us -> none
    all_to_all x0 -> x12, blocking collectives: none -> 219 us  [the longest x6 119 us: sum_parts(): return jnp.sum(lax.all_to_all(parts, axis, 0, 0).astype(f32), axis=0)]
    all_gather x6 -> x0, blocking collectives: 190 us -> none  [the longest x3 124 us: widen_rows(): return lax.all_gather(vector, 'col', axis=1, tiled=True)]
    dot_general x14 -> x0, matrix products: 72.5 us -> none  [the longest x3 21.8 us: forward(): jnp.einsum('ckj,kij->cki', gathered, local_tiles, preferred_element_type=...]
  transfers between devices with their start and end apart: 8 -> 1, of which waited for: 8 -> 1; matrix products, arithmetic and copies ran while one was open for 1% -> 0% of each run, Pallas kernels for 0% -> 0%
where the time goes in v1:
time: 267 us; the launch traced here: 264 us
  blocking collectives  219 us (82%)
  local copies, waits for them, and re-layouts  13.7 us (5%)
  Pallas kernels  11.6 us (4%)
  waiting for transfers between devices  9.34 us (3%)
  starting transfers between devices  7.63 us (3%)
    all_to_all x6, blocking collectives, sum_parts(): return jnp.sum(lax.all_to_all(parts, axis, 0, 0).astype(f32), axis=0)  119 us
    all_to_all x6, blocking collectives, to_all(): lax.all_to_all(jnp.broadcast_to(block[None], (parts, *block.shape)), axis...  99.8 us
    unnamed x18, local copies, waits for them, and re-layouts  13.3 us
    pallas_call x7, Pallas kernels, spread_tiles(): pl.pallas_call(functools.partial(spread_kernel, transposed, degree_rows),...  11.6 us
    all_to_all x1, waiting for transfers between devices, sum_parts(): return jnp.sum(lax.all_to_all(parts, axis, 0, 0).astype(f32), axis=0)  9.34 us
    all_to_all x1, starting transfers between devices, sum_parts(): return jnp.sum(lax.all_to_all(parts, axis, 0, 0).astype(f32), axis=0)  7.63 us
  transfers between devices with their start and end apart: 1, of which 1 were waited for; matrix products, arithmetic and copies ran while one was open for 0% of the time, Pallas kernels for 0%

profile of v1, /device:TPU:8, one launch (start us, length us, event | category | flops | bytes accessed | tf_op | source)
XLA Modules:
  0.0 264.2 jit_solution(3035350127491542279)
XLA Ops:
  0.6 0.0 copy-start.4
  0.6 0.0 copy-start.6
  0.7 0.0 copy-start.7
  1.4 0.0 copy-start
  1.4 4.0 %copy-done = bf16[1,1,80,256,256]{4,3,2,1,0:T(8,128)(2,1)S(1)} copy-done((bf16[1,1,80,256,256]{4,3,2,1,0:T(8,128)(2,1)S(1)}, bf16[1,1,80,256,256]{4,3,2,1,0:T(8,128)(2,1)}, u32[]{:S(2)}) %copy-start) | copy-done | bytes 10485784
  5.4 0.0 copy-start.3
  5.4 0.7 copy-done.3
  6.0 0.0 copy-start.5
  6.0 0.7 copy-done.5
  6.7 1.2 shard_map.68
  7.9 11.5 %all_to_all.65 = f32[16,8,256]{2,1,0:T(8,128)S(1)} all-to-all(f32[16,8,256]{2,1,0:T(8,128)S(1)} %slice.24), channel_id=1, replica_groups=mesh['row'=16,'col'=16] {'row'}, dimensions={0} | all-to-all | bytes 262144 | tf_op jit(solution)/shard_map/all_to_all | solution.py:86
  19.4 0.0 copy-done.7
  19.5 13.1 %all_to_all.66 = bf16[16,64,256]{2,1,0:T(8,128)(2,1)S(1)} all-to-all(bf16[16,64,256]{2,1,0:T(8,128)(2,1)S(1)} %broadcast_in_dim.12), channel_id=1, replica_groups=mesh['row'=16,'col'=16] {'row'}, dimensions={0} | all-to-all | bytes 1048576 | tf_op jit(solution)/shard_map/all_to_all | solution.py:83
  32.7 0.0 copy-done.4
  32.7 0.0 copy-done.6
  32.7 0.0 copy-start.1
  32.7 4.0 %copy-done.1 = bf16[1,1,80,256,256]{4,3,2,1,0:T(8,128)(2,1)S(1)} copy-done((bf16[1,1,80,256,256]{4,3,2,1,0:T(8,128)(2,1)S(1)}, bf16[1,1,80,256,256]{4,3,2,1,0:T(8,128)(2,1)}, u32[]{:S(2)}) %copy-start.1) | copy-done | bytes 10485784
  36.7 1.9 shard_map.69
  38.6 31.7 %all_to_all.67 = bf16[16,80,256]{2,1,0:T(8,128)(2,1)S(1)} all-to-all(bf16[16,80,256]{2,1,0:T(8,128)(2,1)S(1)} %shard_map.69), channel_id=1, replica_groups=mesh['row'=16,'col'=16] {'col'}, dimensions={0} | all-to-all | bytes 1310720 | tf_op jit(solution)/shard_map/all_to_all | solution.py:86
  70.3 0.1 convert_reduce_fusion
  70.5 19.1 %all_to_all.68.source_ref = bf16[16,64,256]{2,1,0:T(8,128)(2,1)S(1)} all-to-all(bf16[16,64,256]{2,1,0:T(8,128)(2,1)S(1)} %broadcast_in_dim.13), channel_id=1, replica_groups=mesh['row'=16,'col'=16] {'col'}, dimensions={0} | all-to-all | bytes 1048576 | tf_op jit(solution)/shard_map/all_to_all | solution.py:83
  89.6 2.2 shard_map.70
  91.8 7.6 %all-to-all-start.4 = ((bf16[16,64,256]{2,1,0:T(8,128)(2,1)}), bf16[16,64,256]{2,1,0:T(8,128)(2,1)S(1)}, u32[]{:S(2)}, u32[]{:S(2)}) async-start(bf16[16,64,256]{2,1,0:T(8,128)(2,1)} %shard_map.70), calls=%async_computation.4 | async-start | bytes 1048576 | tf_op jit(solution)/shard_map/all_to_all | solution.py:86
  99.4 9.3 %all-to-all-done.4 = bf16[16,64,256]{2,1,0:T(8,128)(2,1)S(1)} async-done(((bf16[16,64,256]{2,1,0:T(8,128)(2,1)}), bf16[16,64,256]{2,1,0:T(8,128)(2,1)S(1)}, u32[]{:S(2)}, u32[]{:S(2)}) %all-to-all-start.4) | async-done | bytes 524320 | tf_op jit(solution)/shard_map/all_to_all | solution.py:86
  108.8 0.1 convert_reduce_fusion.5
  108.9 13.5 %all_to_all.69.source_ref = bf16[16,64,256]{2,1,0:T(8,128)(2,1)S(1)} all-to-all(bf16[16,64,256]{2,1,0:T(8,128)(2,1)S(1)} %broadcast_in_dim.14), channel_id=1, replica_groups=mesh['row'=16,'col'=16] {'row'}, dimensions={0} | all-to-all | bytes 1048576 | tf_op jit(solution)/shard_map/all_to_all | solution.py:83
  122.4 0.0 copy-start.2
  122.4 4.0 %copy-done.2 = bf16[1,1,80,256,256]{4,3,2,1,0:T(8,128)(2,1)S(1)} copy-done((bf16[1,1,80,256,256]{4,3,2,1,0:T(8,128)(2,1)S(1)}, bf16[1,1,80,256,256]{4,3,2,1,0:T(8,128)(2,1)}, u32[]{:S(2)}) %copy-start.2) | copy-done | bytes 10485784
  126.4 1.8 shard_map.71
  128.2 21.5 %all_to_all.70 = bf16[16,64,256]{2,1,0:T(8,128)(2,1)S(1)} all-to-all(bf16[16,64,256]{2,1,0:T(8,128)(2,1)S(1)} %shard_map.71), channel_id=1, replica_groups=mesh['row'=16,'col'=16] {'col'}, dimensions={0} | all-to-all | bytes 1048576 | tf_op jit(solution)/shard_map/all_to_all | solution.py:86
  149.7 0.1 convert_reduce_fusion.4
  149.9 20.2 %all_to_all.71.source_ref = bf16[16,64,256]{2,1,0:T(8,128)(2,1)S(1)} all-to-all(bf16[16,64,256]{2,1,0:T(8,128)(2,1)S(1)} %broadcast_in_dim.15), channel_id=1, replica_groups=mesh['row'=16,'col'=16] {'col'}, dimensions={0} | all-to-all | bytes 1048576 | tf_op jit(solution)/shard_map/all_to_all | solution.py:83
  170.1 1.4 shard_map.72
  171.4 16.0 %all_to_all.72 = bf16[16,64,256]{2,1,0:T(8,128)(2,1)S(1)} all-to-all(bf16[16,64,256]{2,1,0:T(8,128)(2,1)S(1)} %shard_map.72), channel_id=1, replica_groups=mesh['row'=16,'col'=16] {'row'}, dimensions={0} | all-to-all | bytes 1048576 | tf_op jit(solution)/shard_map/all_to_all | solution.py:86
  187.4 0.1 convert_reduce_fusion.3
  187.5 0.0 copy-start.8
  187.6 13.4 %all_to_all.73.source_ref = bf16[16,64,256]{2,1,0:T(8,128)(2,1)S(1)} all-to-all(bf16[16,64,256]{2,1,0:T(8,128)(2,1)S(1)} %broadcast_in_dim.16), channel_id=1, replica_groups=mesh['row'=16,'col'=16] {'row'}, dimensions={0} | all-to-all | bytes 1048576 | tf_op jit(solution)/shard_map/all_to_all | solution.py:83
  201.0 1.8 shard_map.73
  202.8 23.3 %all_to_all.74 = bf16[16,64,256]{2,1,0:T(8,128)(2,1)S(1)} all-to-all(bf16[16,64,256]{2,1,0:T(8,128)(2,1)S(1)} %shard_map.73), channel_id=1, replica_groups=mesh['row'=16,'col'=16] {'col'}, dimensions={0} | all-to-all | bytes 1048576 | tf_op jit(solution)/shard_map/all_to_all | solution.py:86
  226.1 0.1 convert_reduce_fusion.2
  226.3 20.5 %all_to_all.75.source_ref = bf16[16,64,256]{2,1,0:T(8,128)(2,1)S(1)} all-to-all(bf16[16,64,256]{2,1,0:T(8,128)(2,1)S(1)} %broadcast_in_dim.17), channel_id=1, replica_groups=mesh['row'=16,'col'=16] {'col'}, dimensions={0} | all-to-all | bytes 1048576 | tf_op jit(solution)/shard_map/all_to_all | solution.py:83
  246.7 1.4 shard_map.74
  248.1 15.3 %all_to_all.76 = bf16[16,64,256]{2,1,0:T(8,128)(2,1)S(1)} all-to-all(bf16[16,64,256]{2,1,0:T(8,128)(2,1)S(1)} %shard_map.74), channel_id=1, replica_groups=mesh['row'=16,'col'=16] {'row'}, dimensions={0} | all-to-all | bytes 1048576 | tf_op jit(solution)/shard_map/all_to_all | solution.py:86
  263.4 0.1 convert_reduce_fusion.1
  263.5 0.0 copy-done.8
  263.5 0.7 multiply_subtract_fusion
  (19 shorter events, 0.4 us)
Async XLA Ops:
  0.6 32.1 %copy-start.4 = (s32[1,1,80]{2,1,0:T(1,128)S(1)}, s32[1,1,80]{2,1,0:T(1,128)}, u32[]{:S(2)}) copy-start(s32[1,1,80]{2,1,0:T(1,128)} %param.7) | copy-start | bytes 964
  0.6 32.1 %copy-start.6 = (s32[1,1,80]{2,1,0:T(1,128)S(1)}, s32[1,1,80]{2,1,0:T(1,128)}, u32[]{:S(2)}) copy-start(s32[1,1,80]{2,1,0:T(1,128)} %param.8) | copy-start | bytes 964
  0.7 18.8 %copy-start.7 = (f32[64,256]{1,0:T(8,128)S(1)}, f32[64,256]{1,0:T(8,128)}, u32[]{:S(2)}) copy-start(f32[64,256]{1,0:T(8,128)} %param.5) | copy-start | bytes 196612
  1.4 4.0 %copy-start = (bf16[1,1,80,256,256]{4,3,2,1,0:T(8,128)(2,1)S(1)}, bf16[1,1,80,256,256]{4,3,2,1,0:T(8,128)(2,1)}, u32[]{:S(2)}) copy-start(bf16[1,1,80,256,256]{4,3,2,1,0:T(8,128)(2,1)} %param.6) | copy-start | bytes 31457284
  5.4 0.7 copy-start.3
  6.0 0.7 copy-start.5
  32.7 4.0 %copy-start.1 = (bf16[1,1,80,256,256]{4,3,2,1,0:T(8,128)(2,1)S(1)}, bf16[1,1,80,256,256]{4,3,2,1,0:T(8,128)(2,1)}, u32[]{:S(2)}) copy-start(bf16[1,1,80,256,256]{4,3,2,1,0:T(8,128)(2,1)} %param.6) | copy-start | bytes 31457284
  91.8 17.0 %all-to-all-start.4 = ((bf16[16,64,256]{2,1,0:T(8,128)(2,1)}), bf16[16,64,256]{2,1,0:T(8,128)(2,1)S(1)}, u32[]{:S(2)}, u32[]{:S(2)}) async-start(bf16[16,64,256]{2,1,0:T(8,128)(2,1)} %shard_map.70), calls=%async_computation.4 | async-start | bytes 1048576 | tf_op jit(solution)/shard_map/all_to_all | solution.py:86
  122.4 4.0 %copy-start.2 = (bf16[1,1,80,256,256]{4,3,2,1,0:T(8,128)(2,1)S(1)}, bf16[1,1,80,256,256]{4,3,2,1,0:T(8,128)(2,1)}, u32[]{:S(2)}) copy-start(bf16[1,1,80,256,256]{4,3,2,1,0:T(8,128)(2,1)} %param.6) | copy-start | bytes 31457284
  187.5 76.0 %copy-start.8 = (f32[64,256]{1,0:T(8,128)}, f32[64,256]{1,0:T(8,128)S(1)}, u32[]{:S(2)}) copy-start(f32[64,256]{1,0:T(8,128)S(1)} %get-tuple-element.3) | copy-start | bytes 196612

commit v2 on v1

v2 whole, which is shorter than its diff:
```python
import functools
import math

import jax
import jax.numpy as jnp
from jax import lax
from jax.experimental import pallas as pl
from jax.experimental.pallas import tpu as pltpu
from jax.sharding import PartitionSpec as P

DEGREE = 3
GROUP = 16
LOAD = 8
AHEAD = 6
EXTRA = 8
FINE = 512.0

filter_center = 0.4
filter_half = 0.4

f16, bf16, f32 = jnp.float16, jnp.bfloat16, jnp.float32
SMEM = pl.BlockSpec(memory_space=pltpu.SMEM)
VMEM = pl.BlockSpec(memory_space=pltpu.VMEM)
HBM = pl.BlockSpec(memory_space=pltpu.HBM)


def halves_of(sums):
    high = sums.astype(bf16).astype(f32)
    return high, (sums - high) * FINE


def load_kernel(
    count_in, rows_in, cols_in, start_in, tiles_ref, held_ref, sent_ref, count_ref, rows_ref, cols_ref,
    start_ref, total_ref, done, read,
):
    slots, width = tiles_ref.shape[0], tiles_ref.shape[2]
    vectors, cover = start_ref.shape[0], total_ref.shape[0]
    pairs = ((start_in, start_ref), (count_in, count_ref), (cols_in, cols_ref), (rows_in, rows_ref))
    small = [pltpu.make_async_copy(*pair, read.at[place]) for place, pair in enumerate(pairs)]
    large = [
        pltpu.make_async_copy(tiles_ref.at[pl.ds(first, LOAD)], held_ref.at[pl.ds(first, LOAD)], done.at[place])
        for place, first in enumerate(range(0, slots, LOAD))
    ]
    for copy in small + large[:AHEAD]:
        copy.start()
    for copy in small:
        copy.wait()
    count = count_ref[0, 0]
    start = start_ref[...]
    largest = jnp.max(jnp.max(jnp.abs(start), axis=0, keepdims=True), axis=1, keepdims=True)
    exponent = jnp.ceil(jnp.log2(jnp.maximum(largest, 1e-30)))
    sent_ref[:vectors] = start * jnp.exp2(-exponent)
    sent_ref[vectors + 2 * cover :] = jnp.broadcast_to(exponent, (EXTRA, width))
    ones = jnp.ones((16, width), bf16)
    for place, copy in enumerate(large):
        copy.wait()
        if place + AHEAD < len(large):
            large[place + AHEAD].start()
        first = place * LOAD
        terms = [jnp.dot(ones, held_ref[first + i], preferred_element_type=f32)[:8] for i in range(LOAD)]
        for slot, term in enumerate(terms, first):
            if slot < cover:
                total_ref[slot] = term
            else:
                total_ref[cols_ref[0, 0, slot]] += jnp.where(slot < count, term, 0.0)
    for place in range(cover):
        high, low = halves_of(total_ref[place, :1])
        sent_ref[vectors + place : vectors + place + 1] = high
        sent_ref[vectors + cover + place : vectors + cover + place + 1] = low


def load(count, rows, cols, start_block, tiles, cover):
    slots, width = tiles.shape[0], tiles.shape[2]
    vectors = start_block.shape[0]
    places = [pltpu.SMEM(array.shape, jnp.int32) for array in (count, rows, cols)]
    sent = jax.ShapeDtypeStruct((vectors + 2 * cover + EXTRA, width), f32)
    operands = [count, rows, cols] + [pltpu.with_memory_space_constraint(array, pltpu.HBM) for array in (start_block, tiles)]
    return pl.pallas_call(
        load_kernel,
        out_shape=(pltpu.VMEM(tiles.shape, bf16), sent, *places),
        in_specs=[HBM] * 5,
        out_specs=(VMEM, VMEM, SMEM, SMEM, SMEM),
        scratch_shapes=[
            pltpu.VMEM(start_block.shape, f32),
            pltpu.VMEM((cover, 8, width), f32),
            pltpu.SemaphoreType.DMA((slots // LOAD,)),
            pltpu.SemaphoreType.DMA((4,)),
        ],
        compiler_params=pltpu.CompilerParams(vmem_limit_bytes=16 * 2**20),
    )(*operands)


def add_products(transposed, count_ref, take_ref, put_ref, source_ref, held_ref, total_ref):
    count, cover = count_ref[0, 0], total_ref.shape[0]
    contract = (((1,), (1 if transposed else 0,)), ((), ()))

    def product(slot, take):
        return lax.dot_general(source_ref[take], held_ref[slot], contract, preferred_element_type=f32)

    for slot in range(cover):
        total_ref[slot] = product(slot, slot)

    def step(group, carry):
        places, terms = [], []
        for offset in range(GROUP):
            slot = group * GROUP + offset
            term = product(slot, take_ref[0, 0, slot])
            places.append(put_ref[0, 0, slot])
            terms.append(jnp.where(slot < count, term, 0.0))
        for place, term in zip(places, terms):
            total_ref[place] += term
        return carry

    lax.fori_loop(cover // GROUP, (count + GROUP - 1) // GROUP, step, 0)


def first_kernel(
    down, count_ref, take_ref, put_ref, mine_ref, theirs_ref, held_ref, out_ref, scale_ref,
    source_ref, total_ref,
):
    cover, width = total_ref.shape[0], total_ref.shape[2]
    vectors = out_ref.shape[1] - EXTRA
    position = lax.axis_index("row")
    core = lax.rem(position, 2)
    degrees, top = jnp.zeros((cover, width), f32), None
    for place in range(cover // 2):
        pair = mine_ref[place, vectors:] + theirs_ref[place, vectors:]
        degrees += pair[:cover] + pair[cover : 2 * cover] * (1.0 / FINE)
        larger = jnp.maximum(mine_ref[place, vectors + 2 * cover :], theirs_ref[place, vectors + 2 * cover :])
        top = larger if top is None else jnp.maximum(top, larger)
    scales = lax.rsqrt(degrees)
    scales = scales * (1.5 - 0.5 * degrees * scales * scales)
    index = lax.broadcasted_iota(jnp.int32, scales.shape, 0)
    scale_ref[...] = jnp.sum(jnp.where(index == position, scales, 0.0), axis=0, keepdims=True)
    for place in range(cover // 2):
        for other, ref in ((0, mine_ref), (1, theirs_ref)):
            odd = jnp.where(core == 1, 1 - other, other)
            scale = jnp.where(odd == 1, scales[2 * place + 1 : 2 * place + 2], scales[2 * place : 2 * place + 1])
            factor = scale * jnp.exp2(ref[place, vectors + 2 * cover :] - top)[:1]
            source_ref[2 * place + odd, :vectors] = (ref[place, :vectors] * factor).astype(bf16)
            source_ref[2 * place + odd, vectors:] = jnp.ones((16, width), bf16)
    add_products(True, count_ref, take_ref, put_ref, source_ref, held_ref, total_ref)
    out_ref[:, :vectors] = total_ref[:, :vectors] * down
    row = lax.broadcasted_iota(jnp.int32, (EXTRA, width), 0)
    for place in range(cover):
        high, low = halves_of(total_ref[place, vectors : vectors + EXTRA])
        out_ref[place, vectors:] = jnp.where(
            row == 0, high, jnp.where(row == 1, low, jnp.where(row == 2, top, 0.0))
        )


def first_product(count, take, put, mine, theirs, held, vectors, down):
    cover, width = mine.shape[0] * 2, mine.shape[2]
    return pl.pallas_call(
        functools.partial(first_kernel, down),
        out_shape=(
            jax.ShapeDtypeStruct((cover, vectors + EXTRA, width), f32),
            jax.ShapeDtypeStruct((1, width), f32),
        ),
        in_specs=[SMEM, SMEM, SMEM, VMEM, VMEM, VMEM],
        out_specs=(VMEM, VMEM),
        scratch_shapes=[
            pltpu.VMEM((cover, vectors + 16, width), bf16),
            pltpu.VMEM((cover, vectors + 16, width), f32),
        ],
        compiler_params=pltpu.CompilerParams(vmem_limit_bytes=16 * 2**20),
    )(count, take, put, mine, theirs, held)


def forward_kernel(
    down, count_ref, take_ref, put_ref, mine_ref, theirs_ref, held_ref, out_ref,
    source_ref, total_ref,
):
    core = lax.rem(lax.axis_index("row"), 2)
    for place in range(total_ref.shape[0] // 2):
        source_ref[2 * place + core] = mine_ref[place]
        source_ref[2 * place + 1 - core] = theirs_ref[place]
    add_products(True, count_ref, take_ref, put_ref, source_ref, held_ref, total_ref)
    out_ref[...] = total_ref[...] * down


def forward(count, take, put, mine, theirs, held, down):
    total = (mine.shape[0] * 2, *mine.shape[1:])
    return pl.pallas_call(
        functools.partial(forward_kernel, down),
        out_shape=jax.ShapeDtypeStruct(total, f32),
        in_specs=[SMEM, SMEM, SMEM, VMEM, VMEM, VMEM],
        out_specs=VMEM,
        scratch_shapes=[pltpu.VMEM(total, bf16), pltpu.VMEM(total, f32)],
        compiler_params=pltpu.CompilerParams(vmem_limit_bytes=16 * 2**20),
    )(count, take, put, mine, theirs, held)


def backward_kernel(
    down, count_ref, take_ref, put_ref, source_ref, held_ref, keep_ref, give_ref,
    total_ref,
):
    core = lax.rem(lax.axis_index("row"), 2)
    add_products(False, count_ref, take_ref, put_ref, source_ref, held_ref, total_ref)
    for place in range(total_ref.shape[0] // 2):
        keep_ref[place] = total_ref[2 * place + core] * down
        give_ref[place] = total_ref[2 * place + 1 - core] * down


def backward(count, take, put, source, held, down):
    half = jax.ShapeDtypeStruct((source.shape[0] // 2, *source.shape[1:]), f32)
    return pl.pallas_call(
        functools.partial(backward_kernel, down),
        out_shape=(half, half),
        in_specs=[SMEM, SMEM, SMEM, VMEM, VMEM],
        out_specs=(VMEM, VMEM),
        scratch_shapes=[pltpu.VMEM(source.shape, f32)],
        compiler_params=pltpu.CompilerParams(vmem_limit_bytes=16 * 2**20),
    )(count, take, put, source, held)


def on_device(start_block, tile_values, rows, cols, count):
    vectors, piece = start_block.shape
    tiles = tile_values[0, 0]
    slots, width = tiles.shape[0], tiles.shape[2]
    row_parts, col_parts = lax.axis_size("col"), lax.axis_size("row")
    chips = col_parts // 2
    same_core = [[2 * chip + core for chip in range(chips)] for core in range(2)]
    swap = [(index, index ^ 1) for index in range(col_parts)]

    nodes = piece * row_parts * col_parts
    longest = 2 * (slots - col_parts + 1) * width
    down = 2.0 ** math.floor(math.log2(60000.0 / (3.5 * math.sqrt(nodes * longest))))

    def over_chips(parts):
        return lax.all_to_all(parts, "row", 0, 0, axis_index_groups=same_core)

    def over_col(parts):
        return lax.all_to_all(parts, "col", 0, 0)

    def copies(block, parts):
        return jnp.broadcast_to(block[None], (parts, *block.shape))

    def other_core(block):
        return lax.ppermute(block, "row", swap)

    def add_parts(parts):
        return jnp.sum(parts.astype(f32), axis=0) * (1.0 / down)

    held, sent, count, rows, cols = load(count, rows, cols, start_block, tiles, col_parts)
    mine = over_chips(copies(sent.astype(f16), chips))
    theirs = other_core(mine)

    partial, col_scale = first_product(count, cols, rows, mine.astype(f32), theirs.astype(f32), held, vectors, down)
    parts = over_col(partial.astype(f16))
    rest = parts[:, vectors:].astype(f32)
    row_inverse = 1.0 / jnp.sum(rest[:, 0] + rest[:, 1] * (1.0 / FINE), axis=0)
    exponent = jnp.max(rest[:, 2], axis=0)
    factors = jnp.exp2(rest[:, 2] - exponent)
    mixed = add_parts(parts[:, :vectors].astype(f32) * factors[:, None])

    previous = current = None
    for index in range(DEGREE):
        if index:
            mine = over_chips(copies((col_scale * current).astype(bf16), chips))
            partial = forward(count, cols, rows, mine, other_core(mine), held, down)
            mixed = add_parts(over_col(partial.astype(f16)))
        weighted = (mixed * row_inverse).astype(bf16)
        keep, give = backward(count, rows, cols, over_col(copies(weighted, row_parts)), held, down)
        parts = over_chips((keep + other_core(give)).astype(f16))
        if index:
            parts, current, previous, exponent = lax.optimization_barrier((parts, current, previous, exponent))
        else:
            parts, sent, exponent, col_scale = lax.optimization_barrier((parts, sent, exponent, col_scale))
            current = sent[:vectors] * jnp.exp2(sent[vectors + 2 * col_parts] - exponent)
        following = (col_scale * add_parts(parts) - filter_center * current) / filter_half
        if index:
            following = 2.0 * following - previous
        previous, current = current, following
    up = jnp.exp2(exponent)
    return current * up, previous * up


def solution(mesh):
    return jax.shard_map(
        on_device,
        mesh=mesh,
        in_specs=(
            P(None, ("col", "row")),
            P("row", "col", None, None, None),
            P("row", "col", None),
            P("row", "col", None),
            P("row", "col"),
        ),
        out_specs=(P(None, ("col", "row")), P(None, ("col", "row"))),
        check_vma=False,
    )
```

time: 267 us -> 235 us (0.88); the launches traced: 264 us -> 236 us
  local copies, waits for them, and re-layouts: 13.7 us -> 1.51 us
  blocking collectives: 219 us -> 207 us
  starting transfers between devices: 7.63 us -> 0.29 us
    all_to_all x12, blocking collectives: 219 us -> 207 us  [the longest x6 140 us: over_col(): return lax.all_to_all(parts, 'col', 0, 0)]
    unnamed x18 -> x5, local copies, waits for them, and re-layouts: 13.3 us -> 1.31 us
    ppermute x0 -> x6, waiting for transfers between devices: none -> 10.5 us  [other_core(): return lax.ppermute(block, 'row', swap)]
    all_to_all x1 -> x0, waiting for transfers between devices: 9.34 us -> none  [sum_parts(): return jnp.sum(lax.all_to_all(parts, axis, 0, 0).astype(f32), axis=0)]
    all_to_all x1 -> x0, starting transfers between devices: 7.63 us -> none  [sum_parts(): return jnp.sum(lax.all_to_all(parts, axis, 0, 0).astype(f32), axis=0)]
  transfers between devices with their start and end apart: 1 -> 6, of which waited for: 1 -> 6; matrix products, arithmetic and copies ran while one was open for 0% -> 0% of each run, Pallas kernels for 0% -> 0%
where the time goes in v2:
time: 235 us; the launch traced here: 236 us
  blocking collectives  207 us (88%)
  Pallas kernels  12.9 us (5%)
  waiting for transfers between devices  10.5 us (4%)
    all_to_all x6, blocking collectives, over_col(): return lax.all_to_all(parts, 'col', 0, 0)  140 us
    all_to_all x6, blocking collectives, over_chips(): return lax.all_to_all(parts, 'row', 0, 0, axis_index_groups=same_core)  66.7 us
    ppermute x6, waiting for transfers between devices, other_core(): return lax.ppermute(block, 'row', swap)  10.5 us
  transfers between devices with their start and end apart: 6, of which 6 were waited for; matrix products, arithmetic and copies ran while one was open for 0% of the time, Pallas kernels for 0%

profile of v2, /device:TPU:8, one launch (start us, length us, event | category | flops | bytes accessed | tf_op | source)
XLA Modules:
  0.0 235.6 jit_solution(15928311652449155578)
XLA Ops:
  1.3 0.0 copy-start
  1.3 0.6 copy-done
  1.9 0.0 copy-start.1
  1.9 0.7 copy-done.1
  2.6 4.6 %shard_map.68 = (bf16[80,256,256]{2,1,0:T(8,128)(2,1)S(1)}, f32[104,256]{1,0:T(8,128)S(1)}, s32[1,1]{1,0:T(1,128)S(4)}, s32[1,1,80]{2,1,0:T(1,128)S(4)}, s32[1,1,80]{2,1,0:T(1,128)S(4)}) custom-call(s32[1,1]{1,0:T(1,128)S(6)} %copy.10.count_in, s32[1,1,80]{2,1,0:T(1,128)S(1)} %copy-done, s32[1,1,80]{2,1,0:T(1,128)S(1)} %copy-done.1, f32[64,256]{1,0:T(8,128)} %start_in.1, ...), custom_call_target="tpu_custom_call" | custom-call | tf_op jit(solution)/shard_map/pallas_call | solution.py:78
  7.3 13.4 %all_to_all.60 = f16[8,104,256]{2,1,0:T(8,128)(2,1)S(1)} all-to-all(f16[8,104,256]{2,1,0:T(8,128)(2,1)S(1)} %broadcast_in_dim.12), channel_id=1, replica_groups={{0,32,64,96,128,160,192,224},{16,48,80,112,144,176,208,240},{1,33,65,97..., dimensions={0} | all-to-all | bytes 851968 | tf_op jit(solution)/shard_map/all_to_all | solution.py:231
  20.7 0.0 collective-permute-start
  20.7 0.1 convert_element_type.76.mine_ref
  20.8 1.7 collective-permute-done
  22.5 0.1 convert_element_type.77.theirs_ref
  22.5 1.7 shard_map.69
  24.2 0.1 convert_element_type.78
  24.3 31.6 %all_to_all.61 = f16[16,72,256]{2,1,0:T(8,128)(2,1)S(1)} all-to-all(f16[16,72,256]{2,1,0:T(8,128)(2,1)S(1)} %convert_element_type.78), channel_id=1, replica_groups=mesh['row'=16,'col'=16] {'col'}, dimensions={0} | all-to-all | bytes 1179648 | tf_op jit(solution)/shard_map/all_to_all | solution.py:234
  55.9 0.1 fusion.1
  56.1 0.1 multiply_reduce_fusion
  56.2 19.7 %all_to_all.62.source_ref = bf16[16,64,256]{2,1,0:T(8,128)(2,1)S(1)} all-to-all(bf16[16,64,256]{2,1,0:T(8,128)(2,1)S(1)} %broadcast_in_dim.13), channel_id=1, replica_groups=mesh['row'=16,'col'=16] {'col'}, dimensions={0} | all-to-all | bytes 1048576 | tf_op jit(solution)/shard_map/all_to_all | solution.py:234
  76.0 1.1 shard_map.70
  77.0 0.1 collective-permute-start.1
  77.1 1.9 collective-permute-done.1
  79.0 0.1 add_convert_fusion.2
  79.1 11.4 %all_to_all.63 = f16[8,64,256]{2,1,0:T(8,128)(2,1)S(1)} all-to-all(f16[8,64,256]{2,1,0:T(8,128)(2,1)S(1)} %add_convert_fusion.2), channel_id=1, replica_groups={{0,32,64,96,128,160,192,224},{16,48,80,112,144,176,208,240},{1,33,65,97..., dimensions={0} | all-to-all | bytes 524288 | tf_op jit(solution)/shard_map/all_to_all | solution.py:231
  90.6 9.8 %all_to_all.64.mine_ref = bf16[8,64,256]{2,1,0:T(8,128)(2,1)S(1)} all-to-all(bf16[8,64,256]{2,1,0:T(8,128)(2,1)S(1)} %broadcast_in_dim.14), channel_id=1, replica_groups={{0,32,64,96,128,160,192,224},{16,48,80,112,144,176,208,240},{1,33,65,97..., dimensions={0} | all-to-all | bytes 524288 | tf_op jit(solution)/shard_map/all_to_all | solution.py:231
  100.5 0.0 collective-permute-start.2
  100.5 1.5 collective-permute-done.2.theirs_ref
  102.0 1.6 shard_map.71
  103.6 0.1 convert_element_type.85
  103.7 23.1 %all_to_all.65 = f16[16,64,256]{2,1,0:T(8,128)(2,1)S(1)} all-to-all(f16[16,64,256]{2,1,0:T(8,128)(2,1)S(1)} %convert_element_type.85), channel_id=1, replica_groups=mesh['row'=16,'col'=16] {'col'}, dimensions={0} | all-to-all | bytes 1048576 | tf_op jit(solution)/shard_map/all_to_all | solution.py:234
  126.9 0.1 convert_reduce_fusion.1
  127.0 21.7 %all_to_all.66.source_ref = bf16[16,64,256]{2,1,0:T(8,128)(2,1)S(1)} all-to-all(bf16[16,64,256]{2,1,0:T(8,128)(2,1)S(1)} %broadcast_in_dim.15), channel_id=1, replica_groups=mesh['row'=16,'col'=16] {'col'}, dimensions={0} | all-to-all | bytes 1048576 | tf_op jit(solution)/shard_map/all_to_all | solution.py:234
  148.7 1.1 shard_map.72
  149.8 0.1 collective-permute-start.3
  149.9 1.9 collective-permute-done.3
  151.8 0.1 add_convert_fusion.1
  151.9 10.6 %all_to_all.67 = f16[8,64,256]{2,1,0:T(8,128)(2,1)S(1)} all-to-all(f16[8,64,256]{2,1,0:T(8,128)(2,1)S(1)} %add_convert_fusion.1), channel_id=1, replica_groups={{0,32,64,96,128,160,192,224},{16,48,80,112,144,176,208,240},{1,33,65,97..., dimensions={0} | all-to-all | bytes 524288 | tf_op jit(solution)/shard_map/all_to_all | solution.py:231
  162.6 9.8 %all_to_all.68.mine_ref = bf16[8,64,256]{2,1,0:T(8,128)(2,1)S(1)} all-to-all(bf16[8,64,256]{2,1,0:T(8,128)(2,1)S(1)} %broadcast_in_dim.16), channel_id=1, replica_groups={{0,32,64,96,128,160,192,224},{16,48,80,112,144,176,208,240},{1,33,65,97..., dimensions={0} | all-to-all | bytes 524288 | tf_op jit(solution)/shard_map/all_to_all | solution.py:231
  172.5 0.0 collective-permute-start.4
  172.5 1.5 collective-permute-done.4.theirs_ref
  174.0 1.8 shard_map.73
  175.8 0.1 convert_element_type.91
  175.9 22.9 %all_to_all.69 = f16[16,64,256]{2,1,0:T(8,128)(2,1)S(1)} all-to-all(f16[16,64,256]{2,1,0:T(8,128)(2,1)S(1)} %convert_element_type.91), channel_id=1, replica_groups=mesh['row'=16,'col'=16] {'col'}, dimensions={0} | all-to-all | bytes 1048576 | tf_op jit(solution)/shard_map/all_to_all | solution.py:234
  198.8 0.1 convert_reduce_fusion
  199.0 21.1 %all_to_all.70.source_ref = bf16[16,64,256]{2,1,0:T(8,128)(2,1)S(1)} all-to-all(bf16[16,64,256]{2,1,0:T(8,128)(2,1)S(1)} %broadcast_in_dim.17), channel_id=1, replica_groups=mesh['row'=16,'col'=16] {'col'}, dimensions={0} | all-to-all | bytes 1048576 | tf_op jit(solution)/shard_map/all_to_all | solution.py:234
  220.1 1.1 shard_map.74
  221.2 0.1 collective-permute-start.5
  221.3 1.9 collective-permute-done.5
  223.1 0.1 add_convert_fusion
  223.2 11.7 %all_to_all.71 = f16[8,64,256]{2,1,0:T(8,128)(2,1)S(1)} all-to-all(f16[8,64,256]{2,1,0:T(8,128)(2,1)S(1)} %add_convert_fusion), channel_id=1, replica_groups={{0,32,64,96,128,160,192,224},{16,48,80,112,144,176,208,240},{1,33,65,97..., dimensions={0} | all-to-all | bytes 524288 | tf_op jit(solution)/shard_map/all_to_all | solution.py:231
  234.9 0.7 broadcast_multiply_fusion
  (23 shorter events, 0.5 us)
Async XLA Ops:
  1.3 0.7 copy-start
  1.9 0.7 copy-start.1
  20.7 1.8 collective-permute-start
  77.0 2.0 collective-permute-start.1
  100.5 1.5 collective-permute-start.2
  149.8 2.0 collective-permute-start.3
  172.5 1.5 collective-permute-start.4
  221.2 2.0 collective-permute-start.5

commit v3 on v2

--- a/solution.py
+++ b/solution.py
@@ -9,7 +9,7 @@
 from jax.sharding import PartitionSpec as P
 
 DEGREE = 3
-GROUP = 16
+GROUP = 32
 LOAD = 8
 AHEAD = 6
 EXTRA = 8
@@ -74,7 +74,7 @@
     vectors = start_block.shape[0]
     places = [pltpu.SMEM(array.shape, jnp.int32) for array in (count, rows, cols)]
     sent = jax.ShapeDtypeStruct((vectors + 2 * cover + EXTRA, width), f32)
-    operands = [count, rows, cols] + [pltpu.with_memory_space_constraint(array, pltpu.HBM) for array in (start_block, tiles)]
+    operands = [count] + [pltpu.with_memory_space_constraint(array, pltpu.HBM) for array in (rows, cols, start_block, tiles)]
     return pl.pallas_call(
         load_kernel,
         out_shape=(pltpu.VMEM(tiles.shape, bf16), sent, *places),
@@ -90,12 +90,15 @@
     )(*operands)
 
 
-def add_products(transposed, count_ref, take_ref, put_ref, source_ref, held_ref, total_ref):
+def add_products(count_ref, take_ref, put_ref, source_ref, held_ref, total_ref, turned_ref=None):
     count, cover = count_ref[0, 0], total_ref.shape[0]
-    contract = (((1,), (1 if transposed else 0,)), ((), ()))
 
     def product(slot, take):
-        return lax.dot_general(source_ref[take], held_ref[slot], contract, preferred_element_type=f32)
+        tile = held_ref[slot]
+        if turned_ref is not None:
+            tile = tile.T
+            turned_ref[slot] = tile
+        return jnp.dot(source_ref[take], tile, preferred_element_type=f32)
 
     for slot in range(cover):
         total_ref[slot] = product(slot, slot)
@@ -103,7 +106,7 @@
     def step(group, carry):
         places, terms = [], []
         for offset in range(GROUP):
-            slot = group * GROUP + offset
+            slot = cover + group * GROUP + offset
             term = product(slot, take_ref[0, 0, slot])
             places.append(put_ref[0, 0, slot])
             terms.append(jnp.where(slot < count, term, 0.0))
@@ -111,15 +114,16 @@
             total_ref[place] += term
         return carry
 
-    lax.fori_loop(cover // GROUP, (count + GROUP - 1) // GROUP, step, 0)
+    lax.fori_loop(0, (count - cover + GROUP - 1) // GROUP, step, 0)
 
 
 def first_kernel(
-    down, count_ref, take_ref, put_ref, mine_ref, theirs_ref, held_ref, out_ref, scale_ref,
+    down, count_ref, take_ref, put_ref, mine_ref, theirs_ref, held_ref, out_ref, scale_ref, turned_ref,
     source_ref, total_ref,
 ):
     cover, width = total_ref.shape[0], total_ref.shape[2]
-    vectors = out_ref.shape[1] - EXTRA
+    half = width // 2
+    vectors = (out_ref.shape[1] - EXTRA) // 2
     position = lax.axis_index("row")
     core = lax.rem(position, 2)
     degrees, top = jnp.zeros((cover, width), f32), None
@@ -139,14 +143,17 @@
             factor = scale * jnp.exp2(ref[place, vectors + 2 * cover :] - top)[:1]
             source_ref[2 * place + odd, :vectors] = (ref[place, :vectors] * factor).astype(bf16)
             source_ref[2 * place + odd, vectors:] = jnp.ones((16, width), bf16)
-    add_products(True, count_ref, take_ref, put_ref, source_ref, held_ref, total_ref)
-    out_ref[:, :vectors] = total_ref[:, :vectors] * down
-    row = lax.broadcasted_iota(jnp.int32, (EXTRA, width), 0)
+    add_products(count_ref, take_ref, put_ref, source_ref, held_ref, total_ref, turned_ref)
+    row = lax.broadcasted_iota(jnp.int32, (EXTRA, half), 0)
+    for part in range(2):
+        lanes = pl.ds(part * half, half)
+        out_ref[:, part * vectors : (part + 1) * vectors] = total_ref[:, :vectors, lanes] * down
     for place in range(cover):
-        high, low = halves_of(total_ref[place, vectors : vectors + EXTRA])
-        out_ref[place, vectors:] = jnp.where(
-            row == 0, high, jnp.where(row == 1, low, jnp.where(row == 2, top, 0.0))
-        )
+        rest = top[:, :half]
+        for part in range(2):
+            high, low = halves_of(total_ref[place, vectors : vectors + EXTRA, part * half : (part + 1) * half])
+            rest = jnp.where(row == part, high, jnp.where(row == 2 + part, low, rest))
+        out_ref[place, 2 * vectors :] = rest
 
 
 def first_product(count, take, put, mine, theirs, held, vectors, down):
@@ -154,11 +161,12 @@
     return pl.pallas_call(
         functools.partial(first_kernel, down),
         out_shape=(
-            jax.ShapeDtypeStruct((cover, vectors + EXTRA, width), f32),
+            jax.ShapeDtypeStruct((cover, 2 * vectors + EXTRA, width // 2), f32),
             jax.ShapeDtypeStruct((1, width), f32),
+            pltpu.VMEM(held.shape, bf16),
         ),
         in_specs=[SMEM, SMEM, SMEM, VMEM, VMEM, VMEM],
-        out_specs=(VMEM, VMEM),
+        out_specs=(VMEM, VMEM, VMEM),
         scratch_shapes=[
             pltpu.VMEM((cover, vectors + 16, width), bf16),
             pltpu.VMEM((cover, vectors + 16, width), f32),
@@ -175,7 +183,7 @@
     for place in range(total_ref.shape[0] // 2):
         source_ref[2 * place + core] = mine_ref[place]
         source_ref[2 * place + 1 - core] = theirs_ref[place]
-    add_products(True, count_ref, take_ref, put_ref, source_ref, held_ref, total_ref)
+    add_products(count_ref, take_ref, put_ref, source_ref, held_ref, total_ref)
     out_ref[...] = total_ref[...] * down
 
 
@@ -196,7 +204,7 @@
     total_ref,
 ):
     core = lax.rem(lax.axis_index("row"), 2)
-    add_products(False, count_ref, take_ref, put_ref, source_ref, held_ref, total_ref)
+    add_products(count_ref, take_ref, put_ref, source_ref, held_ref, total_ref)
     for place in range(total_ref.shape[0] // 2):
         keep_ref[place] = total_ref[2 * place + core] * down
         give_ref[place] = total_ref[2 * place + 1 - core] * down
@@ -246,23 +254,27 @@
     mine = over_chips(copies(sent.astype(f16), chips))
     theirs = other_core(mine)
 
-    partial, col_scale = first_product(count, cols, rows, mine.astype(f32), theirs.astype(f32), held, vectors, down)
-    parts = over_col(partial.astype(f16))
-    rest = parts[:, vectors:].astype(f32)
-    row_inverse = 1.0 / jnp.sum(rest[:, 0] + rest[:, 1] * (1.0 / FINE), axis=0)
-    exponent = jnp.max(rest[:, 2], axis=0)
-    factors = jnp.exp2(rest[:, 2] - exponent)
-    mixed = add_parts(parts[:, :vectors].astype(f32) * factors[:, None])
+    partial, col_scale, turned = first_product(
+        count, cols, rows, mine.astype(f32), theirs.astype(f32), held, vectors, down
+    )
+    parts = over_col(partial.astype(f16)).astype(f32)
+    rest = parts[:, 2 * vectors :]
+    wide = [jnp.concatenate([rest[:, 2 * i], rest[:, 2 * i + 1]], axis=1) for i in range(3)]
+    row_inverse = 1.0 / jnp.sum(wide[0] + wide[1] * (1.0 / FINE), axis=0)
+    exponent = jnp.max(wide[2], axis=0)
+    factors = jnp.exp2(wide[2] - exponent)[:, None]
+    whole = jnp.concatenate([parts[:, :vectors], parts[:, vectors : 2 * vectors]], axis=2)
+    mixed = add_parts(whole * factors)
 
     previous = current = None
     for index in range(DEGREE):
         if index:
             mine = over_chips(copies((col_scale * current).astype(bf16), chips))
-            partial = forward(count, cols, rows, mine, other_core(mine), held, down)
+            partial = forward(count, cols, rows, mine, other_core(mine), turned, down)
             mixed = add_parts(over_col(partial.astype(f16)))
         weighted = (mixed * row_inverse).astype(bf16)
         keep, give = backward(count, rows, cols, over_col(copies(weighted, row_parts)), held, down)
-        parts = over_chips((keep + other_core(give)).astype(f16))
+        parts = over_chips((keep + other_core(give.astype(f16)).astype(f32)).astype(f16))
         if index:
             parts, current, previous, exponent = lax.optimization_barrier((parts, current, previous, exponent))
         else:

time: 235 us -> 232 us (0.987)
  blocking collectives: 207 us -> 203 us
    all_to_all x6, blocking collectives: 140 us -> 137 us  [over_col(): return lax.all_to_all(parts, 'col', 0, 0)]
where the time goes in v3:
time: 232 us; the launch traced here: 231 us
  blocking collectives  203 us (88%)
  Pallas kernels  14.3 us (6%)
  waiting for transfers between devices  9.33 us (4%)
    all_to_all x6, blocking collectives, over_col(): return lax.all_to_all(parts, 'col', 0, 0)  137 us
    all_to_all x6, blocking collectives, over_chips(): return lax.all_to_all(parts, 'row', 0, 0, axis_index_groups=same_core)  65.9 us
    ppermute x6, waiting for transfers between devices, other_core(): return lax.ppermute(block, 'row', swap)  9.33 us
  transfers between devices with their start and end apart: 6, of which 6 were waited for; matrix products, arithmetic and copies ran while one was open for 0% of the time, Pallas kernels for 0%

profile of v3, /device:TPU:8, one launch (start us, length us, event | category | flops | bytes accessed | tf_op | source)
XLA Modules:
  0.0 230.5 jit_solution(16909857691540808120)
XLA Ops:
  1.3 4.6 %shard_map.68 = (bf16[80,256,256]{2,1,0:T(8,128)(2,1)S(1)}, f32[104,256]{1,0:T(8,128)S(1)}, s32[1,1]{1,0:T(1,128)S(4)}, s32[1,1,80]{2,1,0:T(1,128)S(4)}, s32[1,1,80]{2,1,0:T(1,128)S(4)}) custom-call(s32[1,1]{1,0:T(1,128)S(6)} %copy.15.count_in, s32[1,1,80]{2,1,0:T(1,128)} %rows_in.1, s32[1,1,80]{2,1,0:T(1,128)} %cols_in.1, f32[64,256]{1,0:T(8,128)} %start_in.1, ...), custom_call_target="tpu_custom_call" | custom-call | tf_op jit(solution)/shard_map/pallas_call | solution.py:78
  6.0 13.4 %all_to_all.60 = f16[8,104,256]{2,1,0:T(8,128)(2,1)S(1)} all-to-all(f16[8,104,256]{2,1,0:T(8,128)(2,1)S(1)} %broadcast_in_dim.12), channel_id=1, replica_groups={{0,32,64,96,128,160,192,224},{16,48,80,112,144,176,208,240},{1,33,65,97..., dimensions={0} | all-to-all | bytes 851968 | tf_op jit(solution)/shard_map/all_to_all | solution.py:239
  19.4 0.0 collective-permute-start
  19.4 0.1 convert_element_type.91.mine_ref
  19.5 1.7 collective-permute-done
  21.1 0.1 convert_element_type.92.theirs_ref
  21.2 2.3 %shard_map.69 = (f32[16,136,128]{2,1,0:T(8,128)S(1)}, f32[1,256]{1,0:T(1,128)S(1)}, bf16[80,256,256]{2,1,0:T(8,128)(2,1)S(1)}) custom-call(s32[1,1]{1,0:T(1,128)S(4)} %get-tuple-element.28.count_ref, s32[1,1,80]{2,1,0:T(1,128)S(4)} %get-tuple-element.30.take_ref.put_ref, s32[1,1,80]{2,1,0:T(1,128)S(4)} %get-tuple-element.29.put_ref.take_ref, ...), custom_call_target="tpu_custom_call" | custom-call | tf_op jit(solution)/shard_map/pallas_call | solution.py:161
  23.6 0.1 convert_element_type.93
  23.6 31.6 %all_to_all.61 = f16[16,136,128]{2,1,0:T(8,128)(2,1)S(1)} all-to-all(f16[16,136,128]{2,1,0:T(8,128)(2,1)S(1)} %convert_element_type.93), channel_id=1, replica_groups=mesh['row'=16,'col'=16] {'col'}, dimensions={0} | all-to-all | bytes 1114112 | tf_op jit(solution)/shard_map/all_to_all | solution.py:242
  55.2 0.1 convert_element_type.94
  55.3 0.1 fusion.4
  55.5 0.1 fusion
  55.7 18.7 %all_to_all.62.source_ref = bf16[16,64,256]{2,1,0:T(8,128)(2,1)S(1)} all-to-all(bf16[16,64,256]{2,1,0:T(8,128)(2,1)S(1)} %broadcast_in_dim.13), channel_id=1, replica_groups=mesh['row'=16,'col'=16] {'col'}, dimensions={0} | all-to-all | bytes 1048576 | tf_op jit(solution)/shard_map/all_to_all | solution.py:242
  74.4 1.5 shard_map.70
  75.9 0.1 collective-permute-start.1
  76.0 1.5 collective-permute-done.1
  77.6 0.1 add_convert_fusion.2
  77.6 9.9 %all_to_all.63 = f16[8,64,256]{2,1,0:T(8,128)(2,1)S(1)} all-to-all(f16[8,64,256]{2,1,0:T(8,128)(2,1)S(1)} %add_convert_fusion.2), channel_id=1, replica_groups={{0,32,64,96,128,160,192,224},{16,48,80,112,144,176,208,240},{1,33,65,97..., dimensions={0} | all-to-all | bytes 524288 | tf_op jit(solution)/shard_map/all_to_all | solution.py:239
  87.7 9.8 %all_to_all.64.mine_ref = bf16[8,64,256]{2,1,0:T(8,128)(2,1)S(1)} all-to-all(bf16[8,64,256]{2,1,0:T(8,128)(2,1)S(1)} %broadcast_in_dim.14), channel_id=1, replica_groups={{0,32,64,96,128,160,192,224},{16,48,80,112,144,176,208,240},{1,33,65,97..., dimensions={0} | all-to-all | bytes 524288 | tf_op jit(solution)/shard_map/all_to_all | solution.py:239
  97.5 0.0 collective-permute-start.2
  97.5 1.5 collective-permute-done.2.theirs_ref
  99.0 1.5 shard_map.71
  100.5 0.1 convert_element_type.101
  100.6 23.0 %all_to_all.65 = f16[16,64,256]{2,1,0:T(8,128)(2,1)S(1)} all-to-all(f16[16,64,256]{2,1,0:T(8,128)(2,1)S(1)} %convert_element_type.101), channel_id=1, replica_groups=mesh['row'=16,'col'=16] {'col'}, dimensions={0} | all-to-all | bytes 1048576 | tf_op jit(solution)/shard_map/all_to_all | solution.py:242
  123.6 0.1 convert_reduce_fusion.1
  123.7 20.1 %all_to_all.66.source_ref = bf16[16,64,256]{2,1,0:T(8,128)(2,1)S(1)} all-to-all(bf16[16,64,256]{2,1,0:T(8,128)(2,1)S(1)} %broadcast_in_dim.15), channel_id=1, replica_groups=mesh['row'=16,'col'=16] {'col'}, dimensions={0} | all-to-all | bytes 1048576 | tf_op jit(solution)/shard_map/all_to_all | solution.py:242
  143.8 1.5 shard_map.72
  145.3 0.1 collective-permute-start.3
  145.4 1.5 collective-permute-done.3
  147.0 0.1 add_convert_fusion.1
  147.0 12.1 %all_to_all.67 = f16[8,64,256]{2,1,0:T(8,128)(2,1)S(1)} all-to-all(f16[8,64,256]{2,1,0:T(8,128)(2,1)S(1)} %add_convert_fusion.1), channel_id=1, replica_groups={{0,32,64,96,128,160,192,224},{16,48,80,112,144,176,208,240},{1,33,65,97..., dimensions={0} | all-to-all | bytes 524288 | tf_op jit(solution)/shard_map/all_to_all | solution.py:239
  159.2 9.8 %all_to_all.68.mine_ref = bf16[8,64,256]{2,1,0:T(8,128)(2,1)S(1)} all-to-all(bf16[8,64,256]{2,1,0:T(8,128)(2,1)S(1)} %broadcast_in_dim.16), channel_id=1, replica_groups={{0,32,64,96,128,160,192,224},{16,48,80,112,144,176,208,240},{1,33,65,97..., dimensions={0} | all-to-all | bytes 524288 | tf_op jit(solution)/shard_map/all_to_all | solution.py:239
  169.0 0.0 collective-permute-start.4
  169.0 1.5 collective-permute-done.4.theirs_ref
  170.5 1.5 shard_map.73
  172.0 0.1 convert_element_type.109
  172.1 22.3 %all_to_all.69 = f16[16,64,256]{2,1,0:T(8,128)(2,1)S(1)} all-to-all(f16[16,64,256]{2,1,0:T(8,128)(2,1)S(1)} %convert_element_type.109), channel_id=1, replica_groups=mesh['row'=16,'col'=16] {'col'}, dimensions={0} | all-to-all | bytes 1048576 | tf_op jit(solution)/shard_map/all_to_all | solution.py:242
  194.4 0.1 convert_reduce_fusion
  194.6 21.2 %all_to_all.70.source_ref = bf16[16,64,256]{2,1,0:T(8,128)(2,1)S(1)} all-to-all(bf16[16,64,256]{2,1,0:T(8,128)(2,1)S(1)} %broadcast_in_dim.17), channel_id=1, replica_groups=mesh['row'=16,'col'=16] {'col'}, dimensions={0} | all-to-all | bytes 1048576 | tf_op jit(solution)/shard_map/all_to_all | solution.py:242
  215.7 1.5 shard_map.74
  217.2 0.1 collective-permute-start.5
  217.3 1.5 collective-permute-done.5
  218.9 0.1 add_convert_fusion
  219.0 10.9 %all_to_all.71 = f16[8,64,256]{2,1,0:T(8,128)(2,1)S(1)} all-to-all(f16[8,64,256]{2,1,0:T(8,128)(2,1)S(1)} %add_convert_fusion), channel_id=1, replica_groups={{0,32,64,96,128,160,192,224},{16,48,80,112,144,176,208,240},{1,33,65,97..., dimensions={0} | all-to-all | bytes 524288 | tf_op jit(solution)/shard_map/all_to_all | solution.py:239
  229.9 0.7 broadcast_multiply_fusion
  (27 shorter events, 0.6 us)
Async XLA Ops:
  19.4 1.8 collective-permute-start
  75.9 1.6 collective-permute-start.1
  97.5 1.5 collective-permute-start.2
  145.3 1.6 collective-permute-start.3
  169.0 1.5 collective-permute-start.4
  217.2 1.6 collective-permute-start.5

commit v4 on v3

--- a/solution.py
+++ b/solution.py
@@ -10,6 +10,7 @@
 
 DEGREE = 3
 GROUP = 32
+SMALL = 8
 LOAD = 8
 AHEAD = 6
 EXTRA = 8
@@ -41,21 +42,28 @@
         pltpu.make_async_copy(tiles_ref.at[pl.ds(first, LOAD)], held_ref.at[pl.ds(first, LOAD)], done.at[place])
         for place, first in enumerate(range(0, slots, LOAD))
     ]
-    for copy in small + large[:AHEAD]:
+    for copy in small + large[: cover // LOAD]:
         copy.start()
     for copy in small:
         copy.wait()
     count = count_ref[0, 0]
+
+    def if_live(place, work):
+        pl.when(place * LOAD < count)(work)
+
+    for place in range(cover // LOAD, AHEAD):
+        if_live(place, large[place].start)
     start = start_ref[...]
     largest = jnp.max(jnp.max(jnp.abs(start), axis=0, keepdims=True), axis=1, keepdims=True)
     exponent = jnp.ceil(jnp.log2(jnp.maximum(largest, 1e-30)))
     sent_ref[:vectors] = start * jnp.exp2(-exponent)
-    sent_ref[vectors + 2 * cover :] = jnp.broadcast_to(exponent, (EXTRA, width))
+    sent_ref[vectors + cover :] = jnp.broadcast_to(exponent, (EXTRA, width))
     ones = jnp.ones((16, width), bf16)
-    for place, copy in enumerate(large):
-        copy.wait()
+
+    def add(place):
+        large[place].wait()
         if place + AHEAD < len(large):
-            large[place + AHEAD].start()
+            if_live(place + AHEAD, large[place + AHEAD].start)
         first = place * LOAD
         terms = [jnp.dot(ones, held_ref[first + i], preferred_element_type=f32)[:8] for i in range(LOAD)]
         for slot, term in enumerate(terms, first):
@@ -63,17 +71,21 @@
                 total_ref[slot] = term
             else:
                 total_ref[cols_ref[0, 0, slot]] += jnp.where(slot < count, term, 0.0)
+
+    for place in range(len(large)):
+        if place * LOAD < cover:
+            add(place)
+        else:
+            if_live(place, functools.partial(add, place))
     for place in range(cover):
-        high, low = halves_of(total_ref[place, :1])
-        sent_ref[vectors + place : vectors + place + 1] = high
-        sent_ref[vectors + cover + place : vectors + cover + place + 1] = low
+        sent_ref[vectors + place : vectors + place + 1] = total_ref[place, :1]
 
 
 def load(count, rows, cols, start_block, tiles, cover):
     slots, width = tiles.shape[0], tiles.shape[2]
     vectors = start_block.shape[0]
     places = [pltpu.SMEM(array.shape, jnp.int32) for array in (count, rows, cols)]
-    sent = jax.ShapeDtypeStruct((vectors + 2 * cover + EXTRA, width), f32)
+    sent = jax.ShapeDtypeStruct((vectors + cover + EXTRA, width), f32)
     operands = [count] + [pltpu.with_memory_space_constraint(array, pltpu.HBM) for array in (rows, cols, start_block, tiles)]
     return pl.pallas_call(
         load_kernel,
@@ -90,7 +102,7 @@
     )(*operands)
 
 
-def add_products(count_ref, take_ref, put_ref, source_ref, held_ref, total_ref, turned_ref=None):
+def add_products(count_ref, take_ref, put_ref, source_ref, held_ref, total_ref, turned_ref=None, order=lambda place: place):
     count, cover = count_ref[0, 0], total_ref.shape[0]
 
     def product(slot, take):
@@ -101,20 +113,23 @@
         return jnp.dot(source_ref[take], tile, preferred_element_type=f32)
 
     for slot in range(cover):
-        total_ref[slot] = product(slot, slot)
-
-    def step(group, carry):
+        total_ref[order(slot)] = product(slot, slot)
+
+    def add(first, group):
         places, terms = [], []
-        for offset in range(GROUP):
-            slot = cover + group * GROUP + offset
+        for offset in range(group):
+            slot = first + offset
             term = product(slot, take_ref[0, 0, slot])
-            places.append(put_ref[0, 0, slot])
+            places.append(order(put_ref[0, 0, slot]))
             terms.append(jnp.where(slot < count, term, 0.0))
         for place, term in zip(places, terms):
             total_ref[place] += term
-        return carry
-
-    lax.fori_loop(0, (count - cover + GROUP - 1) // GROUP, step, 0)
+
+    large = (count - cover + GROUP // 2 - 1) // GROUP
+    after = cover + large * GROUP
+    lax.fori_loop(0, large, lambda index, _: add(cover + index * GROUP, GROUP), None)
+    small = jnp.maximum(count - after + SMALL - 1, 0) // SMALL
+    lax.fori_loop(0, small, lambda index, _: add(after + index * SMALL, SMALL), None)
 
 
 def first_kernel(
@@ -128,9 +143,8 @@
     core = lax.rem(position, 2)
     degrees, top = jnp.zeros((cover, width), f32), None
     for place in range(cover // 2):
-        pair = mine_ref[place, vectors:] + theirs_ref[place, vectors:]
-        degrees += pair[:cover] + pair[cover : 2 * cover] * (1.0 / FINE)
-        larger = jnp.maximum(mine_ref[place, vectors + 2 * cover :], theirs_ref[place, vectors + 2 * cover :])
+        degrees += mine_ref[place, vectors : vectors + cover] + theirs_ref[place, vectors : vectors + cover]
+        larger = jnp.maximum(mine_ref[place, vectors + cover :], theirs_ref[place, vectors + cover :])
         top = larger if top is None else jnp.maximum(top, larger)
     scales = lax.rsqrt(degrees)
     scales = scales * (1.5 - 0.5 * degrees * scales * scales)
@@ -140,14 +154,14 @@
         for other, ref in ((0, mine_ref), (1, theirs_ref)):
             odd = jnp.where(core == 1, 1 - other, other)
             scale = jnp.where(odd == 1, scales[2 * place + 1 : 2 * place + 2], scales[2 * place : 2 * place + 1])
-            factor = scale * jnp.exp2(ref[place, vectors + 2 * cover :] - top)[:1]
+            factor = scale * down * jnp.exp2(ref[place, vectors + cover :] - top)[:1]
             source_ref[2 * place + odd, :vectors] = (ref[place, :vectors] * factor).astype(bf16)
             source_ref[2 * place + odd, vectors:] = jnp.ones((16, width), bf16)
     add_products(count_ref, take_ref, put_ref, source_ref, held_ref, total_ref, turned_ref)
     row = lax.broadcasted_iota(jnp.int32, (EXTRA, half), 0)
     for part in range(2):
         lanes = pl.ds(part * half, half)
-        out_ref[:, part * vectors : (part + 1) * vectors] = total_ref[:, :vectors, lanes] * down
+        out_ref[:, part * vectors : (part + 1) * vectors] = total_ref[:, :vectors, lanes]
     for place in range(cover):
         rest = top[:, :half]
         for part in range(2):
@@ -175,51 +189,45 @@
     )(count, take, put, mine, theirs, held)
 
 
-def forward_kernel(
-    down, count_ref, take_ref, put_ref, mine_ref, theirs_ref, held_ref, out_ref,
-    source_ref, total_ref,
-):
+def forward_kernel(count_ref, take_ref, put_ref, mine_ref, theirs_ref, held_ref, total_ref, source_ref):
     core = lax.rem(lax.axis_index("row"), 2)
     for place in range(total_ref.shape[0] // 2):
         source_ref[2 * place + core] = mine_ref[place]
         source_ref[2 * place + 1 - core] = theirs_ref[place]
     add_products(count_ref, take_ref, put_ref, source_ref, held_ref, total_ref)
-    out_ref[...] = total_ref[...] * down
-
-
-def forward(count, take, put, mine, theirs, held, down):
+
+
+def forward(count, take, put, mine, theirs, held):
     total = (mine.shape[0] * 2, *mine.shape[1:])
     return pl.pallas_call(
-        functools.partial(forward_kernel, down),
+        forward_kernel,
         out_shape=jax.ShapeDtypeStruct(total, f32),
         in_specs=[SMEM, SMEM, SMEM, VMEM, VMEM, VMEM],
         out_specs=VMEM,
-        scratch_shapes=[pltpu.VMEM(total, bf16), pltpu.VMEM(total, f32)],
+        scratch_shapes=[pltpu.VMEM(total, bf16)],
         compiler_params=pltpu.CompilerParams(vmem_limit_bytes=16 * 2**20),
     )(count, take, put, mine, theirs, held)
 
 
-def backward_kernel(
-    down, count_ref, take_ref, put_ref, source_ref, held_ref, keep_ref, give_ref,
-    total_ref,
-):
-    core = lax.rem(lax.axis_index("row"), 2)
-    add_products(count_ref, take_ref, put_ref, source_ref, held_ref, total_ref)
-    for place in range(total_ref.shape[0] // 2):
-        keep_ref[place] = total_ref[2 * place + core] * down
-        give_ref[place] = total_ref[2 * place + 1 - core] * down
-
-
-def backward(count, take, put, source, held, down):
-    half = jax.ShapeDtypeStruct((source.shape[0] // 2, *source.shape[1:]), f32)
-    return pl.pallas_call(
-        functools.partial(backward_kernel, down),
-        out_shape=(half, half),
+def backward_kernel(count_ref, take_ref, put_ref, source_ref, held_ref, total_ref):
+    core, half = lax.rem(lax.axis_index("row"), 2), total_ref.shape[0] // 2
+
+    def order(place):
+        return jnp.where(place % 2 == core, 0, half) + place // 2
+
+    add_products(count_ref, take_ref, put_ref, source_ref, held_ref, total_ref, order=order)
+
+
+def backward(count, take, put, source, held):
+    total = pl.pallas_call(
+        backward_kernel,
+        out_shape=jax.ShapeDtypeStruct(source.shape, f32),
         in_specs=[SMEM, SMEM, SMEM, VMEM, VMEM],
-        out_specs=(VMEM, VMEM),
-        scratch_shapes=[pltpu.VMEM(source.shape, f32)],
+        out_specs=VMEM,
         compiler_params=pltpu.CompilerParams(vmem_limit_bytes=16 * 2**20),
     )(count, take, put, source, held)
+    half = source.shape[0] // 2
+    return total[:half], total[half:]
 
 
 def on_device(start_block, tile_values, rows, cols, count):
@@ -248,7 +256,7 @@
         return lax.ppermute(block, "row", swap)
 
     def add_parts(parts):
-        return jnp.sum(parts.astype(f32), axis=0) * (1.0 / down)
+        return jnp.sum(parts.astype(f32), axis=0)
 
     held, sent, count, rows, cols = load(count, rows, cols, start_block, tiles, col_parts)
     mine = over_chips(copies(sent.astype(f16), chips))
@@ -269,18 +277,18 @@
     previous = current = None
     for index in range(DEGREE):
         if index:
-            mine = over_chips(copies((col_scale * current).astype(bf16), chips))
-            partial = forward(count, cols, rows, mine, other_core(mine), turned, down)
+            mine = over_chips(copies((col_scale * down * current).astype(bf16), chips))
+            partial = forward(count, cols, rows, mine, other_core(mine), turned)
             mixed = add_parts(over_col(partial.astype(f16)))
         weighted = (mixed * row_inverse).astype(bf16)
-        keep, give = backward(count, rows, cols, over_col(copies(weighted, row_parts)), held, down)
+        keep, give = backward(count, rows, cols, over_col(copies(weighted, row_parts)), held)
         parts = over_chips((keep + other_core(give.astype(f16)).astype(f32)).astype(f16))
         if index:
             parts, current, previous, exponent = lax.optimization_barrier((parts, current, previous, exponent))
         else:
             parts, sent, exponent, col_scale = lax.optimization_barrier((parts, sent, exponent, col_scale))
-            current = sent[:vectors] * jnp.exp2(sent[vectors + 2 * col_parts] - exponent)
-        following = (col_scale * add_parts(parts) - filter_center * current) / filter_half
+            current = sent[:vectors] * jnp.exp2(sent[vectors + col_parts] - exponent)
+        following = (col_scale * (1.0 / down) * add_parts(parts) - filter_center * current) / filter_half
         if index:
             following = 2.0 * following - previous
         previous, current = current, following

time: 232 us -> 230 us (level); the launches traced: 231 us -> 232 us
    all_to_all x6, blocking collectives: 65.9 us -> 69.5 us  [over_chips(): return lax.all_to_all(parts, 'row', 0, 0, axis_index_groups=same_core)]
where the time goes in v4:
time: 230 us; the launch traced here: 232 us
  blocking collectives  205 us (89%)
  Pallas kernels  12.8 us (6%)
  waiting for transfers between devices  9.25 us (4%)
    all_to_all x6, blocking collectives, over_col(): return lax.all_to_all(parts, 'col', 0, 0)  136 us
    all_to_all x6, blocking collectives, over_chips(): return lax.all_to_all(parts, 'row', 0, 0, axis_index_groups=same_core)  69.5 us
    ppermute x6, waiting for transfers between devices, other_core(): return lax.ppermute(block, 'row', swap)  9.25 us
  transfers between devices with their start and end apart: 6, of which 6 were waited for; matrix products, arithmetic and copies ran while one was open for 0% of the time, Pallas kernels for 0%

profile of v4, /device:TPU:8, one launch (start us, length us, event | category | flops | bytes accessed | tf_op | source)
XLA Modules:
  0.0 231.5 jit_solution(8566001681287467072)
XLA Ops:
  1.3 3.3 %shard_map.68 = (bf16[80,256,256]{2,1,0:T(8,128)(2,1)S(1)}, f32[88,256]{1,0:T(8,128)S(1)}, s32[1,1]{1,0:T(1,128)S(4)}, s32[1,1,80]{2,1,0:T(1,128)S(4)}, s32[1,1,80]{2,1,0:T(1,128)S(4)}) custom-call(s32[1,1]{1,0:T(1,128)S(6)} %copy.15.count_in, s32[1,1,80]{2,1,0:T(1,128)} %rows_in.1, s32[1,1,80]{2,1,0:T(1,128)} %cols_in.1, f32[64,256]{1,0:T(8,128)} %start_in.1, ...), custom_call_target="tpu_custom_call" | custom-call | tf_op jit(solution)/shard_map/pallas_call | solution.py:90
  4.6 12.8 %all_to_all.60 = f16[8,88,256]{2,1,0:T(8,128)(2,1)S(1)} all-to-all(f16[8,88,256]{2,1,0:T(8,128)(2,1)S(1)} %broadcast_in_dim.12), channel_id=1, replica_groups={{0,32,64,96,128,160,192,224},{16,48,80,112,144,176,208,240},{1,33,65,97..., dimensions={0} | all-to-all | bytes 720896 | tf_op jit(solution)/shard_map/all_to_all | solution.py:247
  17.4 0.0 collective-permute-start
  17.5 1.6 collective-permute-done
  19.2 2.3 %shard_map.69 = (f32[16,136,128]{2,1,0:T(8,128)S(1)}, f32[1,256]{1,0:T(1,128)S(1)}, bf16[80,256,256]{2,1,0:T(8,128)(2,1)S(1)}) custom-call(s32[1,1]{1,0:T(1,128)S(4)} %get-tuple-element.22.count_ref, s32[1,1,80]{2,1,0:T(1,128)S(4)} %get-tuple-element.24.take_ref.put_ref, s32[1,1,80]{2,1,0:T(1,128)S(4)} %get-tuple-element.23.put_ref.take_ref, ...), custom_call_target="tpu_custom_call" | custom-call | tf_op jit(solution)/shard_map/pallas_call | solution.py:175
  21.5 0.1 convert_element_type.87
  21.6 31.1 %all_to_all.61 = f16[16,136,128]{2,1,0:T(8,128)(2,1)S(1)} all-to-all(f16[16,136,128]{2,1,0:T(8,128)(2,1)S(1)} %convert_element_type.87), channel_id=1, replica_groups=mesh['row'=16,'col'=16] {'col'}, dimensions={0} | all-to-all | bytes 1114112 | tf_op jit(solution)/shard_map/all_to_all | solution.py:250
  52.7 0.1 convert_element_type.88
  52.9 0.1 fusion.7
  53.1 0.1 fusion
  53.2 18.7 %all_to_all.62.source_ref = bf16[16,64,256]{2,1,0:T(8,128)(2,1)S(1)} all-to-all(bf16[16,64,256]{2,1,0:T(8,128)(2,1)S(1)} %broadcast_in_dim.13), channel_id=1, replica_groups=mesh['row'=16,'col'=16] {'col'}, dimensions={0} | all-to-all | bytes 1048576 | tf_op jit(solution)/shard_map/all_to_all | solution.py:250
  72.0 1.4 shard_map.70
  73.4 0.1 collective-permute-start.1
  73.5 1.5 collective-permute-done.1
  75.0 0.1 fusion.3
  75.1 12.7 %all_to_all.63 = f16[8,64,256]{2,1,0:T(8,128)(2,1)S(1)} all-to-all(f16[8,64,256]{2,1,0:T(8,128)(2,1)S(1)} %fusion.3), channel_id=1, replica_groups={{0,32,64,96,128,160,192,224},{16,48,80,112,144,176,208,240},{1,33,65,97..., dimensions={0} | all-to-all | bytes 524288 | tf_op jit(solution)/shard_map/all_to_all | solution.py:247
  88.0 9.8 %all_to_all.64.mine_ref = bf16[8,64,256]{2,1,0:T(8,128)(2,1)S(1)} all-to-all(bf16[8,64,256]{2,1,0:T(8,128)(2,1)S(1)} %broadcast_in_dim.14), channel_id=1, replica_groups={{0,32,64,96,128,160,192,224},{16,48,80,112,144,176,208,240},{1,33,65,97..., dimensions={0} | all-to-all | bytes 524288 | tf_op jit(solution)/shard_map/all_to_all | solution.py:247
  97.8 0.0 collective-permute-start.2
  97.8 1.5 collective-permute-done.2.theirs_ref
  99.4 1.4 shard_map.71
  100.8 0.1 convert_element_type.94
  100.9 21.8 %all_to_all.65 = f16[16,64,256]{2,1,0:T(8,128)(2,1)S(1)} all-to-all(f16[16,64,256]{2,1,0:T(8,128)(2,1)S(1)} %convert_element_type.94), channel_id=1, replica_groups=mesh['row'=16,'col'=16] {'col'}, dimensions={0} | all-to-all | bytes 1048576 | tf_op jit(solution)/shard_map/all_to_all | solution.py:250
  122.7 0.1 convert_reduce_fusion.1
  122.8 21.7 %all_to_all.66.source_ref = bf16[16,64,256]{2,1,0:T(8,128)(2,1)S(1)} all-to-all(bf16[16,64,256]{2,1,0:T(8,128)(2,1)S(1)} %broadcast_in_dim.15), channel_id=1, replica_groups=mesh['row'=16,'col'=16] {'col'}, dimensions={0} | all-to-all | bytes 1048576 | tf_op jit(solution)/shard_map/all_to_all | solution.py:250
  144.6 1.6 shard_map.72
  146.2 0.1 collective-permute-start.3
  146.3 1.5 collective-permute-done.3
  147.8 0.1 fusion.2
  147.9 11.6 %all_to_all.67 = f16[8,64,256]{2,1,0:T(8,128)(2,1)S(1)} all-to-all(f16[8,64,256]{2,1,0:T(8,128)(2,1)S(1)} %fusion.2), channel_id=1, replica_groups={{0,32,64,96,128,160,192,224},{16,48,80,112,144,176,208,240},{1,33,65,97..., dimensions={0} | all-to-all | bytes 524288 | tf_op jit(solution)/shard_map/all_to_all | solution.py:247
  159.6 9.8 %all_to_all.68.mine_ref = bf16[8,64,256]{2,1,0:T(8,128)(2,1)S(1)} all-to-all(bf16[8,64,256]{2,1,0:T(8,128)(2,1)S(1)} %broadcast_in_dim.16), channel_id=1, replica_groups={{0,32,64,96,128,160,192,224},{16,48,80,112,144,176,208,240},{1,33,65,97..., dimensions={0} | all-to-all | bytes 524288 | tf_op jit(solution)/shard_map/all_to_all | solution.py:247
  169.4 0.0 collective-permute-start.4
  169.4 1.5 collective-permute-done.4.theirs_ref
  171.0 1.4 shard_map.73
  172.4 0.1 convert_element_type.101
  172.5 21.6 %all_to_all.69 = f16[16,64,256]{2,1,0:T(8,128)(2,1)S(1)} all-to-all(f16[16,64,256]{2,1,0:T(8,128)(2,1)S(1)} %convert_element_type.101), channel_id=1, replica_groups=mesh['row'=16,'col'=16] {'col'}, dimensions={0} | all-to-all | bytes 1048576 | tf_op jit(solution)/shard_map/all_to_all | solution.py:250
  194.1 0.1 convert_reduce_fusion
  194.2 20.8 %all_to_all.70.source_ref = bf16[16,64,256]{2,1,0:T(8,128)(2,1)S(1)} all-to-all(bf16[16,64,256]{2,1,0:T(8,128)(2,1)S(1)} %broadcast_in_dim.17), channel_id=1, replica_groups=mesh['row'=16,'col'=16] {'col'}, dimensions={0} | all-to-all | bytes 1048576 | tf_op jit(solution)/shard_map/all_to_all | solution.py:250
  215.0 1.4 shard_map.74
  216.5 0.1 collective-permute-start.5
  216.6 1.5 collective-permute-done.5
  218.1 0.1 fusion.1
  218.2 12.6 %all_to_all.71 = f16[8,64,256]{2,1,0:T(8,128)(2,1)S(1)} all-to-all(f16[8,64,256]{2,1,0:T(8,128)(2,1)S(1)} %fusion.1), channel_id=1, replica_groups={{0,32,64,96,128,160,192,224},{16,48,80,112,144,176,208,240},{1,33,65,97..., dimensions={0} | all-to-all | bytes 524288 | tf_op jit(solution)/shard_map/all_to_all | solution.py:247
  230.9 0.7 broadcast_multiply_fusion
  (31 shorter events, 0.7 us)
Async XLA Ops:
  17.4 1.7 collective-permute-start
  73.4 1.6 collective-permute-start.1
  97.8 1.5 collective-permute-start.2
  146.2 1.6 collective-permute-start.3
  169.4 1.5 collective-permute-start.4
  216.5 1.6 collective-permute-start.5

commit v5 on v4

--- a/solution.py
+++ b/solution.py
@@ -31,8 +31,8 @@
 
 
 def load_kernel(
-    count_in, rows_in, cols_in, start_in, tiles_ref, held_ref, sent_ref, count_ref, rows_ref, cols_ref,
-    start_ref, total_ref, done, read,
+    count_in, rows_in, cols_in, start_in, tiles_ref, held_ref, turned_ref, sent_ref, count_ref, rows_ref, cols_ref,
+    sorted_ref, start_ref, total_ref, done, read,
 ):
     slots, width = tiles_ref.shape[0], tiles_ref.shape[2]
     vectors, cover = start_ref.shape[0], total_ref.shape[0]
@@ -53,6 +53,16 @@
 
     for place in range(cover // LOAD, AHEAD):
         if_live(place, large[place].start)
+    core = lax.rem(lax.axis_index("row"), 2)
+
+    def sort(slot, numbers):
+        side = jnp.where(cols_ref[0, 0, slot] % 2 == core, 0, 1)
+        sorted_ref[side, jnp.where(side == 0, *numbers)] = slot
+        return numbers[0] + 1 - side, numbers[1] + side
+
+    numbers = lax.fori_loop(cover, count, sort, (0, 0))
+    for side in range(2):
+        sorted_ref[side, slots - cover] = numbers[side]
     start = start_ref[...]
     largest = jnp.max(jnp.max(jnp.abs(start), axis=0, keepdims=True), axis=1, keepdims=True)
     exponent = jnp.ceil(jnp.log2(jnp.maximum(largest, 1e-30)))
@@ -67,6 +77,7 @@
         first = place * LOAD
         terms = [jnp.dot(ones, held_ref[first + i], preferred_element_type=f32)[:8] for i in range(LOAD)]
         for slot, term in enumerate(terms, first):
+            turned_ref[slot] = held_ref[slot].T
             if slot < cover:
                 total_ref[slot] = term
             else:
@@ -85,13 +96,14 @@
     slots, width = tiles.shape[0], tiles.shape[2]
     vectors = start_block.shape[0]
     places = [pltpu.SMEM(array.shape, jnp.int32) for array in (count, rows, cols)]
+    places.append(pltpu.SMEM((2, slots - cover + 1), jnp.int32))
     sent = jax.ShapeDtypeStruct((vectors + cover + EXTRA, width), f32)
     operands = [count] + [pltpu.with_memory_space_constraint(array, pltpu.HBM) for array in (rows, cols, start_block, tiles)]
     return pl.pallas_call(
         load_kernel,
-        out_shape=(pltpu.VMEM(tiles.shape, bf16), sent, *places),
+        out_shape=(pltpu.VMEM(tiles.shape, bf16), pltpu.VMEM(tiles.shape, bf16), sent, *places),
         in_specs=[HBM] * 5,
-        out_specs=(VMEM, VMEM, SMEM, SMEM, SMEM),
+        out_specs=(VMEM, VMEM, VMEM, SMEM, SMEM, SMEM, SMEM),
         scratch_shapes=[
             pltpu.VMEM(start_block.shape, f32),
             pltpu.VMEM((cover, 8, width), f32),
@@ -102,38 +114,66 @@
     )(*operands)
 
 
-def add_products(count_ref, take_ref, put_ref, source_ref, held_ref, total_ref, turned_ref=None, order=lambda place: place):
+def add_products(count_ref, take_ref, put_ref, source_ref, held_ref, total_ref):
     count, cover = count_ref[0, 0], total_ref.shape[0]
 
     def product(slot, take):
-        tile = held_ref[slot]
-        if turned_ref is not None:
-            tile = tile.T
-            turned_ref[slot] = tile
-        return jnp.dot(source_ref[take], tile, preferred_element_type=f32)
+        return jnp.dot(source_ref[take], held_ref[slot], preferred_element_type=f32)
 
     for slot in range(cover):
-        total_ref[order(slot)] = product(slot, slot)
+        total_ref[slot] = product(slot, slot)
 
     def add(first, group):
         places, terms = [], []
         for offset in range(group):
             slot = first + offset
             term = product(slot, take_ref[0, 0, slot])
-            places.append(order(put_ref[0, 0, slot]))
+            places.append(put_ref[0, 0, slot])
             terms.append(jnp.where(slot < count, term, 0.0))
         for place, term in zip(places, terms):
             total_ref[place] += term
 
-    large = (count - cover + GROUP // 2 - 1) // GROUP
-    after = cover + large * GROUP
-    lax.fori_loop(0, large, lambda index, _: add(cover + index * GROUP, GROUP), None)
-    small = jnp.maximum(count - after + SMALL - 1, 0) // SMALL
+    in_steps(cover, count, add)
+
+
+def in_steps(first, end, add):
+    large = (end - first + GROUP // 2 - 1) // GROUP
+    after = first + large * GROUP
+    lax.fori_loop(0, large, lambda index, _: add(first + index * GROUP, GROUP), None)
+    small = jnp.maximum(end - after + SMALL - 1, 0) // SMALL
     lax.fori_loop(0, small, lambda index, _: add(after + index * SMALL, SMALL), None)
 
 
+def add_side(side, sorted_ref, take_ref, put_ref, held_ref, source, total_ref, place, first):
+    core, cover = lax.rem(lax.axis_index("row"), 2), take_ref.shape[2] + 1 - sorted_ref.shape[1]
+    number = sorted_ref[side, sorted_ref.shape[1] - 1]
+
+    def product(slot, take):
+        return jnp.dot(source(take), held_ref[slot], preferred_element_type=f32)
+
+    for index in range(cover // 2):
+        slot = 2 * index + (core if side == 0 else 1 - core)
+        term = product(slot, slot)
+        if first:
+            total_ref[place(slot)] = term
+        else:
+            total_ref[place(slot)] += term
+
+    def add(start, group):
+        places, terms = [], []
+        for offset in range(group):
+            index = start + offset
+            slot = jnp.where(index < number, sorted_ref[side, index], 0)
+            places.append(place(put_ref[0, 0, slot]))
+            terms.append(jnp.where(index < number, product(slot, take_ref[0, 0, slot]), 0.0))
+        for into, term in zip(places, terms):
+            total_ref[into] += term
+
+    in_steps(0, number, add)
+
+
 def first_kernel(
-    down, count_ref, take_ref, put_ref, mine_ref, theirs_ref, held_ref, out_ref, scale_ref, turned_ref,
+    down, count_ref, take_ref, put_ref, mine_ref, theirs_ref, held_ref, out_ref, scale_ref,
     source_ref, total_ref,
 ):
     cover, width = total_ref.shape[0], total_ref.shape[2]
@@ -157,7 +197,7 @@
             factor = scale * down * jnp.exp2(ref[place, vectors + cover :] - top)[:1]
             source_ref[2 * place + odd, :vectors] = (ref[place, :vectors] * factor).astype(bf16)
             source_ref[2 * place + odd, vectors:] = jnp.ones((16, width), bf16)
-    add_products(count_ref, take_ref, put_ref, source_ref, held_ref, total_ref, turned_ref)
+    add_products(count_ref, take_ref, put_ref, source_ref, held_ref, total_ref)
     row = lax.broadcasted_iota(jnp.int32, (EXTRA, half), 0)
     for part in range(2):
         lanes = pl.ds(part * half, half)
@@ -177,10 +217,9 @@
         out_shape=(
             jax.ShapeDtypeStruct((cover, 2 * vectors + EXTRA, width // 2), f32),
             jax.ShapeDtypeStruct((1, width), f32),
-            pltpu.VMEM(held.shape, bf16),
         ),
         in_specs=[SMEM, SMEM, SMEM, VMEM, VMEM, VMEM],
-        out_specs=(VMEM, VMEM, VMEM),
+        out_specs=(VMEM, VMEM),
         scratch_shapes=[
             pltpu.VMEM((cover, vectors + 16, width), bf16),
             pltpu.VMEM((cover, vectors + 16, width), f32),
@@ -189,45 +228,42 @@
     )(count, take, put, mine, theirs, held)
 
 
-def forward_kernel(count_ref, take_ref, put_ref, mine_ref, theirs_ref, held_ref, total_ref, source_ref):
-    core = lax.rem(lax.axis_index("row"), 2)
-    for place in range(total_ref.shape[0] // 2):
-        source_ref[2 * place + core] = mine_ref[place]
-        source_ref[2 * place + 1 - core] = theirs_ref[place]
-    add_products(count_ref, take_ref, put_ref, source_ref, held_ref, total_ref)
-
-
-def forward(count, take, put, mine, theirs, held):
-    total = (mine.shape[0] * 2, *mine.shape[1:])
+def forward_kernel(side, sorted_ref, take_ref, put_ref, source_ref, held_ref, *refs):
+    total_ref, core = refs[-1], lax.rem(lax.axis_index("row"), 2)
+    if side == 0:
+        for index in range(total_ref.shape[0] // 2):
+            total_ref[2 * index + 1 - core] = jnp.zeros(total_ref.shape[1:], f32)
+    add_side(
+        side, sorted_ref, take_ref, put_ref, held_ref, lambda take: source_ref[take // 2], total_ref, lambda p: p, side == 0
+    )
+
+
+def forward(side, places, take, put, source, held, total=None):
+    shape = (source.shape[0] * 2, *source.shape[1:])
     return pl.pallas_call(
-        forward_kernel,
-        out_shape=jax.ShapeDtypeStruct(total, f32),
-        in_specs=[SMEM, SMEM, SMEM, VMEM, VMEM, VMEM],
+        functools.partial(forward_kernel, side),
+        out_shape=jax.ShapeDtypeStruct(shape, f32),
+        in_specs=[SMEM, SMEM, SMEM, VMEM, VMEM] + [VMEM] * side,
         out_specs=VMEM,
-        scratch_shapes=[pltpu.VMEM(total, bf16)],
+        input_output_aliases={5: 0} if side else {},
         compiler_params=pltpu.CompilerParams(vmem_limit_bytes=16 * 2**20),
-    )(count, take, put, mine, theirs, held)
-
-
-def backward_kernel(count_ref, take_ref, put_ref, source_ref, held_ref, total_ref):
-    core, half = lax.rem(lax.axis_index("row"), 2), total_ref.shape[0] // 2
-
-    def order(place):
-        return jnp.where(place % 2 == core, 0, half) + place // 2
-
-    add_products(count_ref, take_ref, put_ref, source_ref, held_ref, total_ref, order=order)
-
-
-def backward(count, take, put, source, held):
-    total = pl.pallas_call(
-        backward_kernel,
-        out_shape=jax.ShapeDtypeStruct(source.shape, f32),
+    )(places, take, put, source, held, *([total] if side else []))
+
+
+def backward_kernel(side, sorted_ref, take_ref, put_ref, source_ref, held_ref, total_ref):
+    add_side(
+        side, sorted_ref, take_ref, put_ref, held_ref, lambda take: source_ref[take], total_ref, lambda p: p // 2, True
+    )
+
+
+def backward(side, places, take, put, source, held):
+    return pl.pallas_call(
+        functools.partial(backward_kernel, side),
+        out_shape=jax.ShapeDtypeStruct((source.shape[0] // 2, *source.shape[1:]), f32),
         in_specs=[SMEM, SMEM, SMEM, VMEM, VMEM],
         out_specs=VMEM,
         compiler_params=pltpu.CompilerParams(vmem_limit_bytes=16 * 2**20),
-    )(count, take, put, source, held)
-    half = source.shape[0] // 2
-    return total[:half], total[half:]
+    )(places, take, put, source, held)
 
 
 def on_device(start_block, tile_values, rows, cols, count):
@@ -258,12 +294,12 @@
     def add_parts(parts):
         return jnp.sum(parts.astype(f32), axis=0)
 
-    held, sent, count, rows, cols = load(count, rows, cols, start_block, tiles, col_parts)
+    held, turned, sent, count, rows, cols, places = load(count, rows, cols, start_block, tiles, col_parts)
     mine = over_chips(copies(sent.astype(f16), chips))
     theirs = other_core(mine)
 
-    partial, col_scale, turned = first_product(
-        count, cols, rows, mine.astype(f32), theirs.astype(f32), held, vectors, down
+    partial, col_scale = first_product(
+        count, cols, rows, mine.astype(f32), theirs.astype(f32), turned, vectors, down
     )
     parts = over_col(partial.astype(f16)).astype(f32)
     rest = parts[:, 2 * vectors :]
@@ -278,11 +314,15 @@
     for index in range(DEGREE):
         if index:
             mine = over_chips(copies((col_scale * down * current).astype(bf16), chips))
-            partial = forward(count, cols, rows, mine, other_core(mine), turned)
+            theirs = other_core(mine)
+            partial = forward(0, places, cols, rows, mine, turned)
+            partial = forward(1, places, cols, rows, theirs, turned, partial)
             mixed = add_parts(over_col(partial.astype(f16)))
         weighted = (mixed * row_inverse).astype(bf16)
-        keep, give = backward(count, rows, cols, over_col(copies(weighted, row_parts)), held)
-        parts = over_chips((keep + other_core(give.astype(f16)).astype(f32)).astype(f16))
+        gathered = over_col(copies(weighted, row_parts))
+        given = other_core(backward(1, places, rows, cols, gathered, held).astype(f16))
+        keep = backward(0, places, rows, cols, gathered, held)
+        parts = over_chips((keep + given.astype(f32)).astype(f16))
         if index:
             parts, current, previous, exponent = lax.optimization_barrier((parts, current, previous, exponent))
         else:

time: 230 us -> 224 us (0.974)
  Pallas kernels: 12.8 us -> 6.15 us
    pallas_call x6 -> x11, Pallas kernels: 10.4 us -> 5.52 us  [the longest x1 2.08 us: load(): pl.pallas_call(load_kernel, out_shape=(pltpu.VMEM(tiles.shape, bf16), plt...]
  transfers between devices with their start and end apart: 6 -> 6, of which waited for: 6 -> 6; matrix products, arithmetic and copies ran while one was open for 0% -> 0% of each run, Pallas kernels for 0% -> 1%
where the time goes in v5:
time: 224 us
  blocking collectives  206 us (92%)
  waiting for transfers between devices  7.42 us (3%)
  Pallas kernels  6.15 us (3%)
    all_to_all x6, blocking collectives, over_col(): return lax.all_to_all(parts, 'col', 0, 0)  137 us
    all_to_all x6, blocking collectives, over_chips(): return lax.all_to_all(parts, 'row', 0, 0, axis_index_groups=same_core)  68.9 us
    ppermute x6, waiting for transfers between devices, other_core(): return lax.ppermute(block, 'row', swap)  7.42 us
  transfers between devices with their start and end apart: 6, of which 6 were waited for; matrix products, arithmetic and copies ran while one was open for 0% of the time, Pallas kernels for 1%

profile of v5, /device:TPU:8, one launch (start us, length us, event | category | flops | bytes accessed | tf_op | source)
XLA Modules:
  0.0 223.8 jit_solution(11772243421940365563)
XLA Ops:
  1.3 2.1 shard_map.68
  3.4 14.5 %all_to_all.60 = f16[8,88,256]{2,1,0:T(8,128)(2,1)S(1)} all-to-all(f16[8,88,256]{2,1,0:T(8,128)(2,1)S(1)} %broadcast_in_dim.12), channel_id=1, replica_groups={{0,32,64,96,128,160,192,224},{16,48,80,112,144,176,208,240},{1,33,65,97..., dimensions={0} | all-to-all | bytes 720896 | tf_op jit(solution)/shard_map/all_to_all | solution.py:283
  17.9 0.0 collective-permute-start
  18.0 1.6 collective-permute-done
  19.6 0.6 shard_map.69
  20.3 0.1 convert_element_type.93
  20.4 31.3 %all_to_all.61 = f16[16,136,128]{2,1,0:T(8,128)(2,1)S(1)} all-to-all(f16[16,136,128]{2,1,0:T(8,128)(2,1)S(1)} %convert_element_type.93), channel_id=1, replica_groups=mesh['row'=16,'col'=16] {'col'}, dimensions={0} | all-to-all | bytes 1114112 | tf_op jit(solution)/shard_map/all_to_all | solution.py:286
  51.6 0.1 convert_element_type.94
  51.7 0.1 fusion.4
  51.9 0.1 fusion
  52.1 17.8 %all_to_all.62.source_ref = bf16[16,64,256]{2,1,0:T(8,128)(2,1)S(1)} all-to-all(bf16[16,64,256]{2,1,0:T(8,128)(2,1)S(1)} %broadcast_in_dim.13), channel_id=1, replica_groups=mesh['row'=16,'col'=16] {'col'}, dimensions={0} | all-to-all | bytes 1048576 | tf_op jit(solution)/shard_map/all_to_all | solution.py:286
  69.9 0.3 shard_map.71
  70.3 0.1 collective-permute-start.1
  70.4 0.3 shard_map.70
  70.7 1.2 collective-permute-done.1
  71.9 0.1 add_convert_fusion.2
  72.0 12.3 %all_to_all.63 = f16[8,64,256]{2,1,0:T(8,128)(2,1)S(1)} all-to-all(f16[8,64,256]{2,1,0:T(8,128)(2,1)S(1)} %add_convert_fusion.2), channel_id=1, replica_groups={{0,32,64,96,128,160,192,224},{16,48,80,112,144,176,208,240},{1,33,65,97..., dimensions={0} | all-to-all | bytes 524288 | tf_op jit(solution)/shard_map/all_to_all | solution.py:283
  84.5 9.8 %all_to_all.64.source_ref = bf16[8,64,256]{2,1,0:T(8,128)(2,1)S(1)} all-to-all(bf16[8,64,256]{2,1,0:T(8,128)(2,1)S(1)} %broadcast_in_dim.14), channel_id=1, replica_groups={{0,32,64,96,128,160,192,224},{16,48,80,112,144,176,208,240},{1,33,65,97..., dimensions={0} | all-to-all | bytes 524288 | tf_op jit(solution)/shard_map/all_to_all | solution.py:283
  94.3 0.0 collective-permute-start.2
  94.3 0.5 shard_map.72.refs_0_
  94.8 1.0 collective-permute-done.2.source_ref
  95.8 0.4 shard_map.73
  96.2 0.1 convert_element_type.101
  96.3 23.3 %all_to_all.65 = f16[16,64,256]{2,1,0:T(8,128)(2,1)S(1)} all-to-all(f16[16,64,256]{2,1,0:T(8,128)(2,1)S(1)} %convert_element_type.101), channel_id=1, replica_groups=mesh['row'=16,'col'=16] {'col'}, dimensions={0} | all-to-all | bytes 1048576 | tf_op jit(solution)/shard_map/all_to_all | solution.py:286
  119.6 0.1 convert_reduce_fusion.1
  119.7 21.1 %all_to_all.66.source_ref = bf16[16,64,256]{2,1,0:T(8,128)(2,1)S(1)} all-to-all(bf16[16,64,256]{2,1,0:T(8,128)(2,1)S(1)} %broadcast_in_dim.15), channel_id=1, replica_groups=mesh['row'=16,'col'=16] {'col'}, dimensions={0} | all-to-all | bytes 1048576 | tf_op jit(solution)/shard_map/all_to_all | solution.py:286
  140.8 0.3 shard_map.75
  141.2 0.1 collective-permute-start.3
  141.3 0.3 shard_map.74
  141.6 1.2 collective-permute-done.3
  142.8 0.1 add_convert_fusion.1
  142.9 11.2 %all_to_all.67 = f16[8,64,256]{2,1,0:T(8,128)(2,1)S(1)} all-to-all(f16[8,64,256]{2,1,0:T(8,128)(2,1)S(1)} %add_convert_fusion.1), channel_id=1, replica_groups={{0,32,64,96,128,160,192,224},{16,48,80,112,144,176,208,240},{1,33,65,97..., dimensions={0} | all-to-all | bytes 524288 | tf_op jit(solution)/shard_map/all_to_all | solution.py:283
  154.2 9.8 %all_to_all.68.source_ref = bf16[8,64,256]{2,1,0:T(8,128)(2,1)S(1)} all-to-all(bf16[8,64,256]{2,1,0:T(8,128)(2,1)S(1)} %broadcast_in_dim.16), channel_id=1, replica_groups={{0,32,64,96,128,160,192,224},{16,48,80,112,144,176,208,240},{1,33,65,97..., dimensions={0} | all-to-all | bytes 524288 | tf_op jit(solution)/shard_map/all_to_all | solution.py:283
  164.0 0.0 collective-permute-start.4
  164.0 0.3 shard_map.76.refs_0_
  164.3 1.2 collective-permute-done.4.source_ref
  165.5 0.3 shard_map.77
  165.9 0.1 convert_element_type.109
  166.0 22.5 %all_to_all.69 = f16[16,64,256]{2,1,0:T(8,128)(2,1)S(1)} all-to-all(f16[16,64,256]{2,1,0:T(8,128)(2,1)S(1)} %convert_element_type.109), channel_id=1, replica_groups=mesh['row'=16,'col'=16] {'col'}, dimensions={0} | all-to-all | bytes 1048576 | tf_op jit(solution)/shard_map/all_to_all | solution.py:286
  188.5 0.1 convert_reduce_fusion
  188.7 21.0 %all_to_all.70.source_ref = bf16[16,64,256]{2,1,0:T(8,128)(2,1)S(1)} all-to-all(bf16[16,64,256]{2,1,0:T(8,128)(2,1)S(1)} %broadcast_in_dim.17), channel_id=1, replica_groups=mesh['row'=16,'col'=16] {'col'}, dimensions={0} | all-to-all | bytes 1048576 | tf_op jit(solution)/shard_map/all_to_all | solution.py:286
  209.7 0.3 shard_map.79
  210.1 0.1 collective-permute-start.5
  210.2 0.3 shard_map.78
  210.5 1.2 collective-permute-done.5
  211.7 0.1 add_convert_fusion
  211.8 11.3 %all_to_all.71 = f16[8,64,256]{2,1,0:T(8,128)(2,1)S(1)} all-to-all(f16[8,64,256]{2,1,0:T(8,128)(2,1)S(1)} %add_convert_fusion), channel_id=1, replica_groups={{0,32,64,96,128,160,192,224},{16,48,80,112,144,176,208,240},{1,33,65,97..., dimensions={0} | all-to-all | bytes 524288 | tf_op jit(solution)/shard_map/all_to_all | solution.py:283
  223.1 0.7 broadcast_multiply_fusion
  (31 shorter events, 0.7 us)
Async XLA Ops:
  17.9 1.7 collective-permute-start
  70.3 1.6 collective-permute-start.1
  94.3 1.5 collective-permute-start.2
  141.2 1.6 collective-permute-start.3
  164.0 1.5 collective-permute-start.4
  210.1 1.6 collective-permute-start.5

commit v6 on v5

--- a/solution.py
+++ b/solution.py
@@ -55,14 +55,16 @@
         if_live(place, large[place].start)
     core = lax.rem(lax.axis_index("row"), 2)
 
-    def sort(slot, numbers):
+    last = slots - cover
+    for side in range(2):
+        sorted_ref[side, last] = 0
+
+    def sort(slot):
         side = jnp.where(cols_ref[0, 0, slot] % 2 == core, 0, 1)
-        sorted_ref[side, jnp.where(side == 0, *numbers)] = slot
-        return numbers[0] + 1 - side, numbers[1] + side
-
-    numbers = lax.fori_loop(cover, count, sort, (0, 0))
-    for side in range(2):
-        sorted_ref[side, slots - cover] = numbers[side]
+        number = sorted_ref[side, last]
+        sorted_ref[side, number] = slot
+        sorted_ref[side, last] = number + jnp.where(slot < count, 1, 0)
+
     start = start_ref[...]
     largest = jnp.max(jnp.max(jnp.abs(start), axis=0, keepdims=True), axis=1, keepdims=True)
     exponent = jnp.ceil(jnp.log2(jnp.maximum(largest, 1e-30)))
@@ -82,6 +84,7 @@
                 total_ref[slot] = term
             else:
                 total_ref[cols_ref[0, 0, slot]] += jnp.where(slot < count, term, 0.0)
+                sort(slot)
 
     for place in range(len(large)):
         if place * LOAD < cover:

time: 224 us -> 224 us (level)
  Pallas kernels: 6.15 us -> 12.5 us
  blocking collectives: 206 us -> 202 us
  waiting for transfers between devices: 7.42 us -> 4.28 us
    all_to_all x6, blocking collectives: 68.9 us -> 64.2 us  [over_chips(): return lax.all_to_all(parts, 'row', 0, 0, axis_index_groups=same_core)]
    ppermute x6, waiting for transfers between devices: 7.42 us -> 4.28 us  [other_core(): return lax.ppermute(block, 'row', swap)]
    pallas_call x6, Pallas kernels: 1.92 us -> 4.79 us  [backward(): pl.pallas_call(functools.partial(backward_kernel, side), out_shape=jax.Sh...]
  transfers between devices with their start and end apart: 6 -> 6, of which waited for: 6 -> 6; matrix products, arithmetic and copies ran while one was open for 0% -> 0% of each run, Pallas kernels for 1% -> 2%
where the time goes in v6:
time: 224 us; the launch traced here: 223 us
  blocking collectives  202 us (90%)
  Pallas kernels  12.5 us (6%)
  waiting for transfers between devices  4.28 us (2%)
    all_to_all x6, blocking collectives, over_col(): return lax.all_to_all(parts, 'col', 0, 0)  138 us
    all_to_all x6, blocking collectives, over_chips(): return lax.all_to_all(parts, 'row', 0, 0, axis_index_groups=same_core)  64.2 us
    pallas_call x6, Pallas kernels, backward(): pl.pallas_call(functools.partial(backward_kernel, side), out_shape=jax.Sh...  4.79 us
  transfers between devices with their start and end apart: 6, of which 6 were waited for; matrix products, arithmetic and copies ran while one was open for 0% of the time, Pallas kernels for 2%

profile of v6, /device:TPU:8, one launch (start us, length us, event | category | flops | bytes accessed | tf_op | source)
XLA Modules:
  0.0 223.4 jit_solution(2868500498407982942)
XLA Ops:
  1.3 3.1 %shard_map.68 = (bf16[80,256,256]{2,1,0:T(8,128)(2,1)S(1)}, bf16[80,256,256]{2,1,0:T(8,128)(2,1)S(1)}, f32[88,256]{1,0:T(8,128)S(1)}, s32[1,1]{1,0:T(1,128)S(4)}...) custom-call(s32[1,1]{1,0:T(1,128)S(6)} %copy.19.count_in, s32[1,1,80]{2,1,0:T(1,128)} %rows_in.1, ...), custom_call_target="tpu_custom_call" | custom-call | tf_op jit(solution)/shard_map/pallas_call | solution.py:105
  4.4 13.4 %all_to_all.60 = f16[8,88,256]{2,1,0:T(8,128)(2,1)S(1)} all-to-all(f16[8,88,256]{2,1,0:T(8,128)(2,1)S(1)} %broadcast_in_dim.12), channel_id=1, replica_groups={{0,32,64,96,128,160,192,224},{16,48,80,112,144,176,208,240},{1,33,65,97..., dimensions={0} | all-to-all | bytes 720896 | tf_op jit(solution)/shard_map/all_to_all | solution.py:286
  17.8 0.0 collective-permute-start
  17.9 1.6 collective-permute-done
  19.6 1.3 shard_map.69
  20.9 0.1 convert_element_type.93
  20.9 31.1 %all_to_all.61 = f16[16,136,128]{2,1,0:T(8,128)(2,1)S(1)} all-to-all(f16[16,136,128]{2,1,0:T(8,128)(2,1)S(1)} %convert_element_type.93), channel_id=1, replica_groups=mesh['row'=16,'col'=16] {'col'}, dimensions={0} | all-to-all | bytes 1114112 | tf_op jit(solution)/shard_map/all_to_all | solution.py:289
  52.0 0.1 convert_element_type.94
  52.1 0.1 fusion.4
  52.3 0.1 fusion
  52.5 19.3 %all_to_all.62.source_ref = bf16[16,64,256]{2,1,0:T(8,128)(2,1)S(1)} all-to-all(bf16[16,64,256]{2,1,0:T(8,128)(2,1)S(1)} %broadcast_in_dim.13), channel_id=1, replica_groups=mesh['row'=16,'col'=16] {'col'}, dimensions={0} | all-to-all | bytes 1048576 | tf_op jit(solution)/shard_map/all_to_all | solution.py:289
  71.8 0.6 shard_map.71
  72.5 0.1 collective-permute-start.1
  72.6 1.0 shard_map.70
  73.5 0.6 collective-permute-done.1
  74.1 0.1 add_convert_fusion.2
  74.2 9.9 %all_to_all.63 = f16[8,64,256]{2,1,0:T(8,128)(2,1)S(1)} all-to-all(f16[8,64,256]{2,1,0:T(8,128)(2,1)S(1)} %add_convert_fusion.2), channel_id=1, replica_groups={{0,32,64,96,128,160,192,224},{16,48,80,112,144,176,208,240},{1,33,65,97..., dimensions={0} | all-to-all | bytes 524288 | tf_op jit(solution)/shard_map/all_to_all | solution.py:286
  84.2 9.8 %all_to_all.64.source_ref = bf16[8,64,256]{2,1,0:T(8,128)(2,1)S(1)} all-to-all(bf16[8,64,256]{2,1,0:T(8,128)(2,1)S(1)} %broadcast_in_dim.14), channel_id=1, replica_groups={{0,32,64,96,128,160,192,224},{16,48,80,112,144,176,208,240},{1,33,65,97..., dimensions={0} | all-to-all | bytes 524288 | tf_op jit(solution)/shard_map/all_to_all | solution.py:286
  94.0 0.0 collective-permute-start.2
  94.0 1.1 shard_map.72.refs_0_
  95.2 0.4 collective-permute-done.2.source_ref
  95.6 0.7 shard_map.73
  96.3 0.1 convert_element_type.101
  96.4 22.4 %all_to_all.65 = f16[16,64,256]{2,1,0:T(8,128)(2,1)S(1)} all-to-all(f16[16,64,256]{2,1,0:T(8,128)(2,1)S(1)} %convert_element_type.101), channel_id=1, replica_groups=mesh['row'=16,'col'=16] {'col'}, dimensions={0} | all-to-all | bytes 1048576 | tf_op jit(solution)/shard_map/all_to_all | solution.py:289
  118.8 0.1 convert_reduce_fusion.1
  118.9 21.8 %all_to_all.66.source_ref = bf16[16,64,256]{2,1,0:T(8,128)(2,1)S(1)} all-to-all(bf16[16,64,256]{2,1,0:T(8,128)(2,1)S(1)} %broadcast_in_dim.15), channel_id=1, replica_groups=mesh['row'=16,'col'=16] {'col'}, dimensions={0} | all-to-all | bytes 1048576 | tf_op jit(solution)/shard_map/all_to_all | solution.py:289
  140.7 0.6 shard_map.75
  141.4 0.1 collective-permute-start.3
  141.5 1.0 shard_map.74
  142.4 0.6 collective-permute-done.3
  143.0 0.1 add_convert_fusion.1
  143.1 10.5 %all_to_all.67 = f16[8,64,256]{2,1,0:T(8,128)(2,1)S(1)} all-to-all(f16[8,64,256]{2,1,0:T(8,128)(2,1)S(1)} %add_convert_fusion.1), channel_id=1, replica_groups={{0,32,64,96,128,160,192,224},{16,48,80,112,144,176,208,240},{1,33,65,97..., dimensions={0} | all-to-all | bytes 524288 | tf_op jit(solution)/shard_map/all_to_all | solution.py:286
  153.6 9.8 %all_to_all.68.source_ref = bf16[8,64,256]{2,1,0:T(8,128)(2,1)S(1)} all-to-all(bf16[8,64,256]{2,1,0:T(8,128)(2,1)S(1)} %broadcast_in_dim.16), channel_id=1, replica_groups={{0,32,64,96,128,160,192,224},{16,48,80,112,144,176,208,240},{1,33,65,97..., dimensions={0} | all-to-all | bytes 524288 | tf_op jit(solution)/shard_map/all_to_all | solution.py:286
  163.5 0.0 collective-permute-start.4
  163.5 0.9 shard_map.76.refs_0_
  164.4 0.6 collective-permute-done.4.source_ref
  165.0 0.7 shard_map.77
  165.7 0.1 convert_element_type.109
  165.8 21.8 %all_to_all.69 = f16[16,64,256]{2,1,0:T(8,128)(2,1)S(1)} all-to-all(f16[16,64,256]{2,1,0:T(8,128)(2,1)S(1)} %convert_element_type.109), channel_id=1, replica_groups=mesh['row'=16,'col'=16] {'col'}, dimensions={0} | all-to-all | bytes 1048576 | tf_op jit(solution)/shard_map/all_to_all | solution.py:289
  187.6 0.1 convert_reduce_fusion
  187.8 21.8 %all_to_all.70.source_ref = bf16[16,64,256]{2,1,0:T(8,128)(2,1)S(1)} all-to-all(bf16[16,64,256]{2,1,0:T(8,128)(2,1)S(1)} %broadcast_in_dim.17), channel_id=1, replica_groups=mesh['row'=16,'col'=16] {'col'}, dimensions={0} | all-to-all | bytes 1048576 | tf_op jit(solution)/shard_map/all_to_all | solution.py:289
  209.5 0.6 shard_map.79
  210.2 0.1 collective-permute-start.5
  210.3 1.0 shard_map.78
  211.3 0.6 collective-permute-done.5
  211.8 0.1 add_convert_fusion
  211.9 10.8 %all_to_all.71 = f16[8,64,256]{2,1,0:T(8,128)(2,1)S(1)} all-to-all(f16[8,64,256]{2,1,0:T(8,128)(2,1)S(1)} %add_convert_fusion), channel_id=1, replica_groups={{0,32,64,96,128,160,192,224},{16,48,80,112,144,176,208,240},{1,33,65,97..., dimensions={0} | all-to-all | bytes 524288 | tf_op jit(solution)/shard_map/all_to_all | solution.py:286
  222.8 0.7 broadcast_multiply_fusion
  (31 shorter events, 0.7 us)
Async XLA Ops:
  17.8 1.7 collective-permute-start
  72.5 1.6 collective-permute-start.1
  94.0 1.5 collective-permute-start.2
  141.4 1.6 collective-permute-start.3
  163.5 1.5 collective-permute-start.4
  210.2 1.6 collective-permute-start.5
